TPU v7x, 256 devices: a whole 4x4x8 slice. The times are simulated.
256 devices in a mesh: section: 4 (over y), shard: 32 (over x_lo, z, core), mp: 2 (over x_hi).
Axes of the slice: x: 4 (x_hi: 2, x_lo: 2; x = x_hi * 2 + x_lo), y: 4, z: 8, core: 2. Of those that a mesh axis runs over, the one named last changes fastest.
Arguments:
- queries: bfloat16 [32768, 1536], P(('section', 'shard'), 'mp'), may hold values from -6 to 6
- ctx_keys: bfloat16 [32768, 1536], P(('section', 'shard'), 'mp'), may hold values from -88 to 88
- ctx_values: bfloat16 [32768, 1536], P(('section', 'shard'), 'mp'), may hold values from -6 to 6
- cotangent: bfloat16 [32768, 1536], P(('section', 'shard'), 'mp'), may hold values from -6 to 6
- owner: int32 [512, 2], P(('section', 'shard')), may hold values from 0 to 31, all different within a row; in each aligned block of 4 rows (0 to 3, 4 to 7, ...) at most 2 rows name the same one
- slot_row: int32 [512, 2], P(('section', 'shard')), may hold values from 0 to 11
- database: bfloat16 [384, 64, 1536], P('shard'), may hold values from -6 to 6
- enc_gain: float32 [1536], replicated, may hold values from 0.25 to 1.75
- enc_query_w: bfloat16 [1536, 1536], P('section', 'mp'), may hold values from -0.15625 to 0.15625
- enc_out_w: bfloat16 [1536, 1536], P('section', 'mp'), may hold values from -0.15625 to 0.15625
Outputs:
- attended: bfloat16 [32768, 1536], P(('section', 'shard'), 'mp')
- grad_queries: bfloat16 [32768, 1536], P(('section', 'shard'), 'mp')
- grad_keys: bfloat16 [32768, 1536], P(('section', 'shard'), 'mp')
- grad_values: bfloat16 [32768, 1536], P(('section', 'shard'), 'mp')
Inputs may be any that keep to these rules, and one draw needn't show every extreme that they name: The 2 owners of one query span differ. Among the rows of one device no owner is named more than 2 times.
All inputs are finite; a program needn't handle non-finite values.
Results may differ from a plain program's by a relative error of at most 0.02.
The roundings to bfloat16 on the way count: a program that leaves them out, or rounds other values in their place, can miss the bound.
Values may be sent and summed in bfloat16 or wider, within the bound.
A program may use at most 128 MiB of HBM per device.

v0:
```python
import jax
import jax.numpy as jnp
from jax import lax
from jax.sharding import PartitionSpec as P

DH = 128
CT = 64
NT = 64
K = 2


def softmax_rows(scores):
    top = jnp.max(scores, axis=-1, keepdims=True)
    weights = jnp.exp(scores - top)
    return weights / jnp.sum(weights, axis=-1, keepdims=True)


def local(
    queries,
    ctx_keys,
    ctx_values,
    cotangent,
    owner,
    slot_row,
    database,
    enc_gain,
    enc_query_w,
    enc_out_w,
):
    half = queries.shape[1]
    width = database.shape[2]
    heads = half // DH
    blocks = owner.shape[0]
    shards = lax.axis_size("shard")
    capacity = max(2, (blocks * K + shards - 1) // shards)
    scale = DH ** (-0.5)
    part = lax.axis_index("mp")
    req_owner = owner.reshape(-1)
    req_row = slot_row.reshape(-1)
    count = req_owner.shape[0]
    order = jnp.arange(count, dtype=jnp.int32)
    earlier = (req_owner[:, None] == req_owner[None, :]) & (order[None, :] < order[:, None])
    rank = jnp.sum(earlier.astype(jnp.int32), axis=1)
    target = req_owner * capacity + rank
    slots = jnp.arange(shards * capacity, dtype=jnp.int32)
    table = (target[:, None] == slots[None, :]).astype(jnp.int32)
    request_rows = jnp.sum(table * req_row[:, None], axis=0).reshape(shards, capacity)
    incoming = lax.all_to_all(request_rows, "shard", split_axis=0, concat_axis=0, tiled=True)
    picked = jnp.take(database, incoming.reshape(-1), axis=0)
    returned = lax.all_to_all(
        picked.reshape(shards, capacity, NT, width),
        "shard",
        split_axis=0,
        concat_axis=0,
        tiled=True,
    )
    fetched = jnp.take(returned.reshape(shards * capacity, NT, width), target, axis=0)
    wide = fetched.reshape(-1, width).astype(jnp.float32)
    squares = jnp.mean(wide * wide, axis=1, keepdims=True)
    normed = (wide * lax.rsqrt(squares + 1e-06) * enc_gain).astype(jnp.bfloat16)
    query_full, out_full = (
        lax.all_gather(enc_query_w, "section", axis=0, tiled=True),
        lax.all_gather(enc_out_w, "section", axis=0, tiled=True),
    )
    enc_q = jnp.dot(normed, query_full, preferred_element_type=jnp.float32).astype(jnp.bfloat16)
    enc_q4 = enc_q.reshape(blocks, K * NT, heads, DH)
    keys4 = ctx_keys.reshape(blocks, CT, heads, DH)
    values4 = ctx_values.reshape(blocks, CT, heads, DH)
    enc_p = softmax_rows(
        jnp.einsum("cqhd,ckhd->chqk", enc_q4, keys4, preferred_element_type=jnp.float32) * scale
    )
    enc_pb = enc_p.astype(jnp.bfloat16)
    mixed = jnp.einsum(
        "chqk,ckhd->cqhd", enc_pb, values4, preferred_element_type=jnp.float32
    ).astype(jnp.bfloat16)
    projected = lax.dot_general(
        mixed.reshape(-1, half),
        out_full,
        (((1,), (1,)), ((), ())),
        preferred_element_type=jnp.float32,
    )
    own_sum = lax.psum_scatter(projected, "mp", scatter_dimension=1, tiled=True)
    residual = lax.dynamic_slice_in_dim(wide, part * half, half, 1)
    encoded = (residual + own_sum).astype(jnp.bfloat16)
    enc4 = encoded.reshape(blocks, K * NT, heads, DH)
    query4 = queries.reshape(blocks, CT, heads, DH)
    cca_p = softmax_rows(
        jnp.einsum("cqhd,ckhd->chqk", query4, enc4, preferred_element_type=jnp.float32) * scale
    )
    cca_pb = cca_p.astype(jnp.bfloat16)
    attended = jnp.einsum(
        "chqk,ckhd->cqhd", cca_pb, enc4, preferred_element_type=jnp.float32
    ).astype(jnp.bfloat16)
    grad4 = cotangent.reshape(blocks, CT, heads, DH)
    d_p = jnp.einsum("cqhd,ckhd->chqk", grad4, enc4, preferred_element_type=jnp.float32)
    d_s = (cca_p * (d_p - jnp.sum(d_p * cca_p, axis=-1, keepdims=True))).astype(jnp.bfloat16)
    grad_queries = (
        scale * jnp.einsum("chqk,ckhd->cqhd", d_s, enc4, preferred_element_type=jnp.float32)
    ).astype(jnp.bfloat16)
    key_part = jnp.einsum("chqk,cqhd->ckhd", d_s, query4, preferred_element_type=jnp.float32)
    value_part = jnp.einsum("chqk,cqhd->ckhd", cca_pb, grad4, preferred_element_type=jnp.float32)
    d_enc = (scale * key_part + value_part).astype(jnp.bfloat16)
    d_full = lax.all_gather(d_enc.reshape(-1, half), "mp", axis=1, tiled=True)
    d_mixed = jnp.dot(d_full, out_full, preferred_element_type=jnp.float32).astype(jnp.bfloat16)
    d_mixed4 = d_mixed.reshape(blocks, K * NT, heads, DH)
    grad_values = jnp.einsum(
        "chqk,cqhd->ckhd", enc_pb, d_mixed4, preferred_element_type=jnp.float32
    ).astype(jnp.bfloat16)
    d_pe = jnp.einsum("cqhd,ckhd->chqk", d_mixed4, values4, preferred_element_type=jnp.float32)
    d_se = (enc_p * (d_pe - jnp.sum(d_pe * enc_p, axis=-1, keepdims=True))).astype(jnp.bfloat16)
    grad_keys = (
        scale * jnp.einsum("chqk,cqhd->ckhd", d_se, enc_q4, preferred_element_type=jnp.float32)
    ).astype(jnp.bfloat16)
    shape = (blocks * CT, half)
    return (
        attended.reshape(shape),
        grad_queries.reshape(shape),
        grad_keys.reshape(shape),
        grad_values.reshape(shape),
    )


def solution(mesh):
    return jax.shard_map(
        local,
        mesh=mesh,
        in_specs=(
            P(("section", "shard"), "mp"),
            P(("section", "shard"), "mp"),
            P(("section", "shard"), "mp"),
            P(("section", "shard"), "mp"),
            P(("section", "shard"), None),
            P(("section", "shard"), None),
            P("shard", None, None),
            P(),
            P("section", "mp"),
            P("section", "mp"),
        ),
        out_specs=(
            P(("section", "shard"), "mp"),
            P(("section", "shard"), "mp"),
            P(("section", "shard"), "mp"),
            P(("section", "shard"), "mp"),
        ),
        check_vma=False,
    )
```

profile of v0, /device:TPU:1, one launch (start us, length us, event | category | flops | bytes accessed | tf_op | source)
XLA Modules:
  0.0 479.6 jit_solution(6081045096958413345)
XLA Ops:
  7.2 0.9 copy.93
  8.1 0.1 reshape.177
  8.2 0.2 convert_reduce_fusion
  8.4 0.8 copy.94
  9.2 0.1 mul.94
  9.2 0.1 select_reduce_fusion
  9.3 0.1 all_to_all.9
  9.4 18.7 %all_to_all.14 = s32[32,1,2]{2,1,0:T(1,128)S(1)} all-to-all(s32[32,1,2]{2,1,0:T(1,128)S(1)} %bitcast.84), channel_id=1, replica_groups=mesh['section'=4,'shard'=32,'mp'=2] {'shard'}, dimensions={0} | all-to-all | bytes 512 | tf_op jit(solution)/shard_map/all_to_all | solution.py:48
  28.1 0.5 broadcast.139
  28.6 0.7 reduce.4
  29.3 0.1 reshape.179
  29.5 0.1 copy.97
  29.7 6.9 %gather_fusion = bf16[64,64,1536]{2,1,0:T(8,128)(2,1)} fusion(bf16[12,64,1536]{2,1,0:T(8,128)(2,1)S(1)} %copy-done, s32[1024]{0:T(1024)S(1)} %pad_clamp_fusion.1), kind=kCustom, calls=%fused_computation | custom fusion | bytes 25166080 | tf_op jit(solution)/shard_map/jit(_take)/gather | solution.py:49
  36.5 10.9 %broadcast_select_fusion = bf16[32,2,64,1536]{3,2,1,0:T(8,128)(2,1)} fusion(bf16[32,2,64,1536]{3,2,1,0:T(8,128)(2,1)} %bitcast.76, pred[32,2]{1,0:T(8,128)(4,1)S(1)} %copy.97), kind=kLoop, calls=%fused_computation.4 | loop fusion | flops 6291456 | bytes 25165888 | tf_op jit(solution)/shard_map/jit(_take)/select_n | solution.py:49
  47.4 5.6 %all-to-all-start.1 = ((bf16[32,2,64,1536]{3,2,1,0:T(8,128)(2,1)}), bf16[32,2,64,1536]{3,2,1,0:T(8,128)(2,1)}, u32[]{:S(2)}, u32[]{:S(2)}) async-start(bf16[32,2,64,1536]{3,2,1,0:T(8,128)(2,1)} %broadcast_select_fusion), calls=%async_computation.1 | async-start | bytes 25165824 | tf_op jit(solution)/shard_map/all_to_all | solution.py:50
  53.0 0.7 all-gather.4.cloned.1.call-update
  53.8 0.7 all-gather.6.cloned.1.call-update
  54.5 0.1 copy.98
  54.6 0.1 mul.98
  54.8 0.1 broadcast_in_dim.41
  54.9 0.5 reshape.182
  55.3 1.3 reshape.183
  56.7 268.9 %all-to-all-done.1 = bf16[32,2,64,1536]{3,2,1,0:T(8,128)(2,1)} async-done(((bf16[32,2,64,1536]{3,2,1,0:T(8,128)(2,1)}), bf16[32,2,64,1536]{3,2,1,0:T(8,128)(2,1)}, u32[]{:S(2)}, u32[]{:S(2)}) %all-to-all-start.1) | async-done | bytes 12582944 | tf_op jit(solution)/shard_map/all_to_all | solution.py:50
  325.6 5.2 %gather_fusion.1 = bf16[8,64,1536]{2,1,0:T(8,128)(2,1)S(1)} fusion(bf16[64,64,1536]{2,1,0:T(8,128)(2,1)} %bitcast.4, s32[1024]{0:T(1024)S(1)} %pad_clamp_fusion), kind=kCustom, calls=%fused_computation.1 | custom fusion | bytes 3145760 | tf_op jit(solution)/shard_map/jit(_take)/gather | solution.py:57
  330.8 0.6 multiply_reduce_fusion
  331.4 0.1 rsqrt.12
  331.5 2.0 fusion.3
  333.5 4.1 fusion.8
  337.6 0.9 reshape.210
  338.5 0.6 convolution_multiply_fusion.3
  339.1 1.2 fusion.48
  340.4 0.5 fusion.9
  340.8 0.6 copy.103
  341.5 4.8 %fusion.20 = f32[512,1536]{1,0:T(8,128)} fusion(bf16[1536,768]{1,0:T(8,128)(2,1)} %all-gather.6.cloned.1.call-done, bf16[96,8,4,128]{3,2,1,0:T(4,128)(2,1)S(1)} %bitcast.83), kind=kOutput, calls=%fused_computation.38 | convolution fusion | flops 1207959552 | bytes 6291456 | tf_op jit(solution)/shard_map/dot_general | solution.py:76
  346.3 0.2 all-gather.8.cloned.1.call-start
  346.6 0.7 copy-done.10
  347.3 0.5 reshape.186
  347.8 1.2 reshape.188
  349.0 53.3 %reduce-scatter.2.cloned.1.call-done = f32[512,768]{1,0:T(8,128)} async-done(((f32[512,1536]{1,0:T(8,128)}), f32[512,768]{1,0:T(8,128)}) %reduce-scatter.2.cloned.1.call-update) | async-done | bytes 1572880 | tf_op jit(solution)/shard_map/reduce_scatter | solution.py:82
  402.3 2.9 add_convert_fusion.1
  405.2 2.0 reshape.211
  407.2 0.6 fusion.13
  407.8 0.9 copy-done.3
  408.7 4.1 fusion.49
  412.9 0.8 multiply_reduce_fusion.2
  413.6 0.5 multiply_convert_fusion.5
  414.1 1.6 fusion.32
  415.7 6.0 %fusion.12 = bf16[4,128,6,128]{3,1,2,0:T(8,128)(2,1)} fusion(f32[4,6,128,128]{3,2,1,0:T(8,128)} %fusion.32, bf16[4,64,6,128]{3,2,1,0:T(8,128)(2,1)} %reshape.188, f32[4,6,64]{2,1,0:T(8,128)S(1)} %get-tuple-element.8, f32[4,6,64,128]{3,2,1,0:T(8,128)} %copy-done.3), kind=kOutput, calls=%fused_computation.23 | convolution fusion | flops 52102784 | bytes 3545088 | tf_op jit(solution)/shard_map/chqk,cqhd->ckhd/dot_general | solution.py:101
  421.8 1.5 copy.115
  423.3 1.0 copy.182
  424.3 4.1 fusion.18
  428.4 0.3 copy.108
  428.7 0.3 fusion.17
  429.1 0.3 copy.112
  429.3 1.0 copy_bitcast_fusion.3
  430.3 27.4 %all-gather.8.cloned.1.call-done = bf16[512,1536]{0,1:T(8,128)(2,1)} async-done(((bf16[512,768]{0,1:T(8,128)(2,1)}), bf16[512,1536]{0,1:T(8,128)(2,1)}) %all-gather.8.cloned.1.call-update) | async-done | bytes 1572880 | tf_op jit(solution)/shard_map/all_gather | solution.py:103
  457.8 3.6 convolution_convert_fusion
  461.4 0.9 reshape.212
  462.3 2.6 fusion.19
  464.9 1.5 multiply_reduce_fusion.1
  466.4 3.0 fusion.16
  469.5 1.3 copy.120
  470.7 1.3 copy.122
  472.0 1.0 copy_bitcast_fusion.1
  (43 shorter events, 0.4 us)
Async XLA Ops:
  7.2 22.5 %copy-start = (bf16[12,64,1536]{2,1,0:T(8,128)(2,1)S(1)}, bf16[12,64,1536]{2,1,0:T(8,128)(2,1)}, u32[]{:S(2)}) copy-start(bf16[12,64,1536]{2,1,0:T(8,128)(2,1)} %param.16) | copy-start | bytes 7077892
  47.4 7.1 %copy-start.12 = (s32[4,2]{0,1:T(2,128)S(1)}, s32[4,2]{0,1:T(2,128)}, u32[]{:S(2)}) copy-start(s32[4,2]{0,1:T(2,128)} %param.14) | copy-start | bytes 100
  47.4 7.5 %copy-start.8 = (bf16[256,768]{1,0:T(8,128)(2,1)S(1)}, bf16[256,768]{1,0:T(8,128)(2,1)}, u32[]{:S(2)}) copy-start(bf16[256,768]{1,0:T(8,128)(2,1)} %param.11) | copy-start | bytes 1179652
  47.4 278.2 %all-to-all-start.1 = ((bf16[32,2,64,1536]{3,2,1,0:T(8,128)(2,1)}), bf16[32,2,64,1536]{3,2,1,0:T(8,128)(2,1)}, u32[]{:S(2)}, u32[]{:S(2)}) async-start(bf16[32,2,64,1536]{3,2,1,0:T(8,128)(2,1)} %broadcast_select_fusion), calls=%async_computation.1 | async-start | bytes 25165824 | tf_op jit(solution)/shard_map/all_to_all | solution.py:50
  53.0 2.4 copy-start.9
  53.0 280.5 %all-gather.4.cloned.1.call-start = ((), (), s32[]{:S(2)}) async-start(), calls=%async_computation.3 | async-start | bytes 2949120 | tf_op jit(solution)/shard_map/all_gather | solution.py:62
  53.7 287.8 %all-gather.6.cloned.1.call-start = ((), (), s32[]{:S(2)}) async-start(), calls=%async_computation.4 | async-start | bytes 2949120 | tf_op jit(solution)/shard_map/all_gather | solution.py:63
  54.5 347.9 %reduce-scatter.2.cloned.1.call-start = ((), (), s32[]{:S(2)}) async-start(), calls=%async_computation.5 | async-start | bytes 4718592 | tf_op jit(solution)/shard_map/reduce_scatter | solution.py:82
  331.5 2.1 copy-start.13
  337.6 2.8 copy-start.5
  339.1 1.7 copy-start.2
  346.3 1.0 copy-start.10
  346.3 1.5 copy-start.11
  346.3 111.5 %all-gather.8.cloned.1.call-start = ((), (), s32[]{:S(2)}) async-start(), calls=%async_computation.6 | async-start | bytes 2359296 | tf_op jit(solution)/shard_map/all_gather | solution.py:103
  407.2 5.7 %copy-start.7 = (bf16[4,64,6,128]{3,2,1,0:T(8,128)(2,1)S(1)}, bf16[4,64,6,128]{3,2,1,0:T(8,128)(2,1)}, u32[]{:S(2)}) copy-start(bf16[4,64,6,128]{3,2,1,0:T(8,128)(2,1)} %reshape.188) | copy-start | bytes 1179652
  407.8 0.9 copy-start.3
  462.3 2.7 copy-start.4
  462.3 2.7 copy-start.6
  466.4 6.6 %copy-start.1 = (bf16[12,64,1536]{2,1,0:T(8,128)(2,1)S(1)}, bf16[12,64,1536]{2,1,0:T(8,128)(2,1)}, u32[]{:S(2)}) copy-start(bf16[12,64,1536]{2,1,0:T(8,128)(2,1)} %param.16) | copy-start | bytes 7077892
Sparse Core Ops, SparseCore 0:
  55.6 36.5 all-gather.3
  94.0 35.6 all-gather.5
  346.4 55.8 reduce-scatter.1
  424.5 33.2 all-gather.7
where the time goes:
time: 480 us
  waiting for transfers between devices  351 us (73%)
  matrix products  34.2 us (7%)
  local copies, waits for them, and re-layouts  32.4 us (7%)
  other arithmetic  23.2 us (5%)
  blocking collectives  18.7 us (4%)
  between operations  14.1 us (3%)
  starting transfers between devices  5.9 us (1%)
    all_to_all x1, waiting for transfers between devices, local(): lax.all_to_all(picked.reshape(shards, capacity, NT, width), 'shard', spli...  269 us
    reduce_scatter x1, waiting for transfers between devices, local(): own_sum = lax.psum_scatter(projected, 'mp', scatter_dimension=1, tiled=True)  53.3 us
    all_gather x1, waiting for transfers between devices, local(): d_full = lax.all_gather(d_enc.reshape(-1, half), 'mp', axis=1, tiled=True)  27.4 us
    all_to_all x1, blocking collectives, local(): lax.all_to_all(request_rows, 'shard', split_axis=0, concat_axis=0, tiled=...  18.7 us
    select_n x2, other arithmetic, local(): picked = jnp.take(database, incoming.reshape(-1), axis=0)  10.9 us
  transfers between devices with their start and end apart: 5, of which 3 were waited for; matrix products, arithmetic and copies ran while one was open for 5% of the time, Pallas kernels for 0%

commit v1 on v0

--- a/solution.py
+++ b/solution.py
@@ -1,12 +1,193 @@
 import jax
 import jax.numpy as jnp
 from jax import lax
+from jax.experimental import pallas as pl
+from jax.experimental.pallas import tpu as pltpu
 from jax.sharding import PartitionSpec as P
 
 DH = 128
 CT = 64
 NT = 64
 K = 2
+MESH = pl.DeviceIdType.MESH
+
+
+def fetch_kernel(req_ref, db_ref, out_ref, rq, rqs, gath, xs, xr, xm,
+                 loc_sem, rq_send, rq_recv, rx_send, rx_recv, sib_send, sib_recv,
+                 zp_send, zp_recv, zm_send, zm_recv, x_send, x_recv, y_send, y_recv, m_send, m_recv):
+    s = lax.axis_index("section")
+    d = lax.axis_index("shard")
+    m = lax.axis_index("mp")
+    x = d // 16
+    z = (d // 2) % 8
+    c = d % 2
+
+    def dev(s_, x_, z_, c_, m_):
+        return (s_, x_ * 16 + z_ * 2 + c_, m_)
+
+    peers = [(ds, dc) for ds in (2, 1, 3, 0) for dc in (0, 1) if (ds, dc) != (0, 0)]
+    zn, zb = (z + 1) % 8, (z + 7) % 8
+
+    def peer(ds, dc):
+        return dev((s + ds) % 4, x, z, (c + dc) % 2, m)
+
+    pair = dev(s, 1 - x, z, c, m)
+    up, down = dev(s, x, zn, c, m), dev(s, x, zb, c, m)
+    mate = dev(s, x, z, c, 1 - m)
+    sib = dev(s, x, z, 1 - c, m)
+
+    barrier = pltpu.get_barrier_semaphore()
+    friends = [peer(*p) for p in peers] + [pair, up, down, mate]
+    for f in friends:
+        pl.semaphore_signal(barrier, inc=1, device_id=f, device_id_type=MESH)
+
+    tok = pl.ds(pl.multiple_of(s * 16, 16), 16)
+    mine = pltpu.make_async_copy(
+        db_ref.at[:, tok, pl.ds(pl.multiple_of((2 * m + c) * 384, 128), 384)],
+        gath.at[pl.ds(z * 24 + c * 12, 12)], loc_sem.at[0])
+    mine.start()
+    me = s * 2 + c
+    own_rq = pltpu.make_async_copy(req_ref, rq.at[x * 8 + me], loc_sem.at[1])
+    own_rq.start()
+    pl.semaphore_wait(barrier, len(friends))
+
+    to_sib = pltpu.make_async_remote_copy(
+        db_ref.at[:, tok, pl.ds(pl.multiple_of((2 * m + 1 - c) * 384, 128), 384)],
+        gath.at[pl.ds(z * 24 + c * 12, 12)], sib_send.at[0], sib_recv.at[0],
+        device_id=sib, device_id_type=MESH)
+    to_sib.start()
+    rq_copies = []
+    for i, (ds, dc) in enumerate(peers):
+        src = ((s + 4 - ds) % 4) * 2 + (c + dc) % 2
+        cp = pltpu.make_async_remote_copy(
+            req_ref, rq.at[x * 8 + me], rq_send.at[i], rq_recv.at[i],
+            device_id=peer(ds, dc), device_id_type=MESH)
+        cp.start()
+        rq_copies.append(cp)
+
+    def zcopy(j, plus):
+        k, h = j // 2, j % 2
+        if k == 3:
+            h = 0 if plus else 1
+        zz = (z + 8 - k) % 8 if plus else (z + k) % 8
+        cls = (c + h) % 2
+        sl = gath.at[pl.ds(zz * 24 + cls * 12, 12)]
+        return pltpu.make_async_remote_copy(
+            sl, sl, (zp_send if plus else zm_send).at[j], (zp_recv if plus else zm_recv).at[j],
+            device_id=up if plus else down, device_id_type=MESH)
+
+    plus, minus = [], []
+    for j in range(7):
+        if j == 0:
+            mine.wait()
+        elif j == 1:
+            to_sib.wait_recv()
+        elif j < 6:
+            plus[j - 2].wait_recv()
+            minus[j - 2].wait_recv()
+        else:
+            plus[4].wait_recv()
+            minus[5].wait_recv()
+        a, b = zcopy(j, True), zcopy(j, False)
+        a.start()
+        b.start()
+        plus.append(a)
+        minus.append(b)
+        if j == 2:
+            own_rq.wait()
+            for cp in rq_copies:
+                cp.wait_recv()
+            fwd = pltpu.make_async_remote_copy(
+                rq.at[pl.ds(x * 8, 8)], rq.at[pl.ds(x * 8, 8)], rx_send.at[0], rx_recv.at[0],
+                device_id=pair, device_id_type=MESH)
+            fwd.start()
+        if j == 4:
+            fwd.wait_recv()
+            to_s = pltpu.make_async_copy(rq, rqs, loc_sem.at[2])
+            to_s.start()
+            to_s.wait()
+    plus[5].wait_recv()
+    plus[6].wait_recv()
+    minus[4].wait_recv()
+    minus[6].wait_recv()
+
+    order = [(ds, dc) for ds in (2, 1, 3, 0) for dc in (0, 1)]
+    xcopies = []
+    for i, (ds, dc) in enumerate(order):
+        dst = ((s + ds) % 4) * 2 + (c + dc) % 2
+        for j in range(8):
+            g = rqs[(1 - x) * 8 + dst, 0, j]
+            xs[i * 8 + j] = gath[lax.rem(g, 192)]
+        cp = pltpu.make_async_remote_copy(
+            xs.at[pl.ds(i * 8, 8)], xr.at[pl.ds(i * 8, 8)], x_send.at[i], x_recv.at[i],
+            device_id=pair, device_id_type=MESH)
+        cp.start()
+        xcopies.append(cp)
+    ycopies = []
+    feat = pl.ds(pl.multiple_of((2 * m + c) * 384, 128), 384)
+    for i, (ds, dc) in enumerate(order):
+        dst = ((s + ds) % 4) * 2 + (c + dc) % 2
+        xcopies[i].wait_recv()
+        for j in range(8):
+            g = rqs[x * 8 + dst, 0, j]
+            own = (g // 192) == x
+            xm[i * 8 + j] = jnp.where(own, gath[lax.rem(g, 192)], xr[i * 8 + j])
+        if (ds, dc) == (0, 0):
+            cp = pltpu.make_async_copy(xm.at[pl.ds(i * 8, 8)], out_ref.at[:, tok, feat], y_recv.at[i])
+        else:
+            cp = pltpu.make_async_remote_copy(
+                xm.at[pl.ds(i * 8, 8)], out_ref.at[:, tok, feat], y_send.at[i], y_recv.at[i],
+                device_id=peer(ds, dc), device_id_type=MESH)
+        cp.start()
+        ycopies.append(cp)
+    mcopies = []
+    for i, (ds, dc) in enumerate(order):
+        if (ds, dc) == (0, 0):
+            ycopies[i].wait()
+        else:
+            ycopies[i].wait_recv()
+        ss, cc = (s + 4 - ds) % 4, (c + dc) % 2
+        piece = out_ref.at[:, pl.ds(pl.multiple_of(ss * 16, 16), 16),
+                           pl.ds(pl.multiple_of((2 * m + cc) * 384, 128), 384)]
+        cp = pltpu.make_async_remote_copy(piece, piece, m_send.at[i], m_recv.at[i],
+                                          device_id=mate, device_id_type=MESH)
+        cp.start()
+        mcopies.append(cp)
+    for cp in mcopies:
+        cp.wait_recv()
+    to_sib.wait_send()
+    fwd.wait_send()
+    for cp in rq_copies + plus + minus + xcopies + mcopies:
+        cp.wait_send()
+    for i, p in enumerate(order):
+        if p != (0, 0):
+            ycopies[i].wait_send()
+
+
+def fetch(req, database):
+    dma = pltpu.SemaphoreType.DMA
+    bf = jnp.bfloat16
+    return pl.pallas_call(
+        fetch_kernel,
+        out_shape=jax.ShapeDtypeStruct((8, 64, 1536), bf),
+        in_specs=[pl.BlockSpec(memory_space=pltpu.VMEM), pl.BlockSpec(memory_space=pl.ANY)],
+        out_specs=pl.BlockSpec(memory_space=pltpu.VMEM),
+        scratch_shapes=[
+            pltpu.VMEM((16, 8, 128), jnp.int32),
+            pltpu.SMEM((16, 8, 128), jnp.int32),
+            pltpu.VMEM((192, 16, 384), bf),
+            pltpu.VMEM((64, 16, 384), bf),
+            pltpu.VMEM((64, 16, 384), bf),
+            pltpu.VMEM((64, 16, 384), bf),
+            dma((3,)),
+            dma((7,)), dma((7,)), dma((1,)), dma((1,)), dma((1,)), dma((1,)),
+            dma((7,)), dma((7,)), dma((7,)), dma((7,)),
+            dma((8,)), dma((8,)), dma((8,)), dma((8,)), dma((8,)), dma((8,)),
+        ],
+        compiler_params=pltpu.CompilerParams(
+            collective_id=0, has_side_effects=True, vmem_limit_bytes=32 * 1024 * 1024),
+        cost_estimate=pl.CostEstimate(flops=0, bytes_accessed=12_000_000, transcendentals=0),
+    )(req, database)
 
 
 def softmax_rows(scores):
@@ -31,30 +212,11 @@
     width = database.shape[2]
     heads = half // DH
     blocks = owner.shape[0]
-    shards = lax.axis_size("shard")
-    capacity = max(2, (blocks * K + shards - 1) // shards)
     scale = DH ** (-0.5)
     part = lax.axis_index("mp")
-    req_owner = owner.reshape(-1)
-    req_row = slot_row.reshape(-1)
-    count = req_owner.shape[0]
-    order = jnp.arange(count, dtype=jnp.int32)
-    earlier = (req_owner[:, None] == req_owner[None, :]) & (order[None, :] < order[:, None])
-    rank = jnp.sum(earlier.astype(jnp.int32), axis=1)
-    target = req_owner * capacity + rank
-    slots = jnp.arange(shards * capacity, dtype=jnp.int32)
-    table = (target[:, None] == slots[None, :]).astype(jnp.int32)
-    request_rows = jnp.sum(table * req_row[:, None], axis=0).reshape(shards, capacity)
-    incoming = lax.all_to_all(request_rows, "shard", split_axis=0, concat_axis=0, tiled=True)
-    picked = jnp.take(database, incoming.reshape(-1), axis=0)
-    returned = lax.all_to_all(
-        picked.reshape(shards, capacity, NT, width),
-        "shard",
-        split_axis=0,
-        concat_axis=0,
-        tiled=True,
-    )
-    fetched = jnp.take(returned.reshape(shards * capacity, NT, width), target, axis=0)
+    wanted = (owner * database.shape[0] + slot_row).reshape(1, -1)
+    request = jnp.pad(wanted, ((0, 7), (0, 128 - wanted.shape[1])))
+    fetched = fetch(request, database)
     wide = fetched.reshape(-1, width).astype(jnp.float32)
     squares = jnp.mean(wide * wide, axis=1, keepdims=True)
     normed = (wide * lax.rsqrt(squares + 1e-06) * enc_gain).astype(jnp.bfloat16)

time: 480 us -> 221 us (0.46)
  waiting for transfers between devices: 351 us -> 76.2 us
  Pallas kernels: 0 us -> 67.3 us
  blocking collectives: 18.7 us -> 0 us
  local copies, waits for them, and re-layouts: 32.4 us -> 18.2 us
  other arithmetic: 23.2 us -> 11.6 us
  starting transfers between devices: 5.9 us -> 0.34 us
    all_to_all x1 -> x0, waiting for transfers between devices: 269 us -> none  [local(): lax.all_to_all(picked.reshape(shards, capacity, NT, width), 'shard', spli...]
    pallas_call x0 -> x1, Pallas kernels: none -> 67.3 us  [fetch(): pl.pallas_call(fetch_kernel, out_shape=jax.ShapeDtypeStruct((8, 64, 1536)...]
    all_to_all x1 -> x0, blocking collectives: 18.7 us -> none  [local(): lax.all_to_all(request_rows, 'shard', split_axis=0, concat_axis=0, tiled=...]
    gather x2 -> x0, local copies, waits for them, and re-layouts: 12.1 us -> none  [the longest x1 6.86 us: local(): picked = jnp.take(database, incoming.reshape(-1), axis=0)]
    select_n x3 -> x0, other arithmetic: 10.9 us -> none  [the longest x2 10.9 us: local(): picked = jnp.take(database, incoming.reshape(-1), axis=0)]
    reduce_scatter x1, waiting for transfers between devices: 53.3 us -> 46 us  [local(): own_sum = lax.psum_scatter(projected, 'mp', scatter_dimension=1, tiled=True)]
    all_to_all x1 -> x0, starting transfers between devices: 5.56 us -> none  [local(): lax.all_to_all(picked.reshape(shards, capacity, NT, width), 'shard', spli...]
  transfers between devices with their start and end apart: 5 -> 4, of which waited for: 3 -> 2; matrix products, arithmetic and copies ran while one was open for 5% -> 10% of each run, Pallas kernels for 0% -> 31%
where the time goes in v1:
time: 221 us; the launch traced here: 220 us
  waiting for transfers between devices  76.2 us (34%)
  Pallas kernels  67.3 us (30%)
  matrix products  32.6 us (15%)
  local copies, waits for them, and re-layouts  18.2 us (8%)
  between operations  14 us (6%)
  other arithmetic  11.6 us (5%)
    pallas_call x1, Pallas kernels, fetch(): pl.pallas_call(fetch_kernel, out_shape=jax.ShapeDtypeStruct((8, 64, 1536)...  67.3 us
    reduce_scatter x1, waiting for transfers between devices, local(): own_sum = lax.psum_scatter(projected, 'mp', scatter_dimension=1, tiled=True)  46 us
    all_gather x1, waiting for transfers between devices, local(): d_full = lax.all_gather(d_enc.reshape(-1, half), 'mp', axis=1, tiled=True)  28.9 us
    dot_general x1, matrix products, local(): jnp.einsum('chqk,cqhd->ckhd', cca_pb, grad4, preferred_element_type=jnp.f...  5.47 us
    sub x2, other arithmetic, softmax_rows(): weights = jnp.exp(scores - top)  5.39 us
    dot_general x1, matrix products, local(): lax.dot_general(mixed.reshape(-1, half), out_full, (((1,), (1,)), ((), ()...  4.81 us
  transfers between devices with their start and end apart: 4, of which 2 were waited for; matrix products, arithmetic and copies ran while one was open for 10% of the time, Pallas kernels for 31%

profile of v1, /device:TPU:1, one launch (start us, length us, event | category | flops | bytes accessed | tf_op | source)
XLA Modules:
  0.0 220.3 jit_solution(17058759937372466855)
XLA Ops:
  7.2 0.0 all-gather.4.cloned.1.call-start
  7.2 0.7 all-gather.4.cloned.1.call-update
  7.9 0.0 all-gather.6.cloned.1.call-start
  7.9 0.7 all-gather.6.cloned.1.call-update
  8.6 0.0 reduce-scatter.2.cloned.1.call-start
  8.7 0.7 multiply_add_fusion
  9.4 0.1 copy.30
  9.5 0.1 reshape.77
  9.6 1.7 copy-done
  11.3 67.3 %shard_map.129 = bf16[8,64,1536]{2,1,0:T(8,128)(2,1)S(1)} custom-call(s32[8,128]{1,0:T(8,128)S(1)} %pad.4.req_ref, bf16[12,64,1536]{2,1,0:T(8,128)(2,1)S(1)} %copy-done), custom_call_target="tpu_custom_call" | custom-call | bytes 12000000 | tf_op jit(solution)/shard_map/pallas_call | solution.py:170
  78.5 0.4 multiply_reduce_fusion
  78.9 0.1 rsqrt.12
  79.0 0.0 copy-done.11
  79.0 0.5 reshape.79
  79.5 0.0 copy-done.12
  79.5 0.5 reshape.80
  80.0 0.0 copy-start.8
  80.0 0.0 copy-start.15
  80.0 2.2 bitcast_convert_fusion
  82.2 0.0 copy-done.15
  82.2 4.1 %fusion.7 = bf16[512,768]{1,0:T(8,128)(2,1)S(1)} fusion(bf16[1536,768]{1,0:T(8,128)(2,1)} %all-gather.4.cloned.1.call-done, f32[512,1536]{1,0:T(8,128)} %bitcast_convert_fusion, f32[1536]{0:T(1024)S(1)} %copy-done.15, f32[512]{0:T(512)S(1)} %rsqrt.12), kind=kOutput, calls=%fused_computation.11 | convolution fusion | flops 1210712064 | bytes 6299648 | tf_op jit(solution)/shard_map/dot_general | solution.py:227
  86.2 0.9 reshape.92
  87.1 0.6 convolution_multiply_fusion.3
  87.8 1.2 fusion.44
  88.9 1.5 fusion.8
  90.4 0.0 copy-done.3
  90.4 1.5 copy.35
  91.9 0.0 all-gather.6.cloned.1.call-done
  92.0 4.8 %fusion.19 = f32[512,1536]{1,0:T(8,128)} fusion(bf16[1536,768]{1,0:T(8,128)(2,1)} %all-gather.6.cloned.1.call-done, bf16[96,8,4,128]{3,2,1,0:T(4,128)(2,1)S(1)} %bitcast.68), kind=kOutput, calls=%fused_computation.33 | convolution fusion | flops 1207959552 | bytes 6291456 | tf_op jit(solution)/shard_map/dot_general | solution.py:238
  96.8 0.0 reduce-scatter.2.cloned.1.call-update
  96.8 0.2 all-gather.8.cloned.1.call-start
  97.0 0.7 copy-done.13
  97.8 1.3 reshape.83
  99.0 2.3 %reshape.85 = bf16[4,64,6,128]{3,2,1,0:T(8,128)(2,1)} reshape(bf16[256,768]{1,0:T(8,128)(2,1)} %param.13) | data formatting | bytes 786432 | tf_op jit(solution)/shard_map/reshape | solution.py:256
  101.3 46.0 %reduce-scatter.2.cloned.1.call-done = f32[512,768]{1,0:T(8,128)} async-done(((f32[512,1536]{1,0:T(8,128)}), f32[512,768]{1,0:T(8,128)}) %reduce-scatter.2.cloned.1.call-update) | async-done | bytes 1572880 | tf_op jit(solution)/shard_map/reduce_scatter | solution.py:244
  147.3 2.5 %add_convert_fusion.1 = bf16[512,768]{1,0:T(8,128)(2,1)} fusion(f32[512,768]{1,0:T(8,128)} %reduce-scatter.2.cloned.1.call-done, f32[512,1536]{1,0:T(8,128)S(1)} %copy-done.1, s32[]{:T(128)S(6)} %select_n.3), kind=kLoop, calls=%fused_computation.6 | loop fusion | flops 786432 | bytes 3932164 | tf_op jit(solution)/shard_map/convert_element_type | solution.py:246
  149.7 2.0 reshape.93
  151.7 1.7 fusion.12
  153.4 4.2 %fusion.45 = (f32[4,6,64]{2,1,0:T(8,128)S(1)}, f32[4,6,64,128]{3,2,1,0:T(8,128)S(1)}) fusion(f32[4,6,64,128]{3,2,1,0:T(8,128)S(1)} %fusion.12), kind=kOutput, calls=%fused_computation.71 | output fusion | flops 393343 | bytes 1579008 | tf_op jit(solution)/shard_map/sub | solution.py:195
  157.6 0.0 copy-done.10
  157.7 0.0 copy-start.2
  157.7 0.8 multiply_reduce_fusion.2
  158.4 0.5 multiply_convert_fusion.5
  158.9 0.0 copy-done.2
  158.9 1.6 fusion.31
  160.5 5.5 %fusion.11 = bf16[4,128,6,128]{3,1,2,0:T(8,128)(2,1)} fusion(f32[4,6,128,128]{3,2,1,0:T(8,128)} %fusion.31, bf16[4,64,6,128]{3,2,1,0:T(8,128)(2,1)S(1)} %copy-done.10, f32[4,6,64]{2,1,0:T(8,128)S(1)} %get-tuple-element.6, f32[4,6,64,128]{3,2,1,0:T(8,128)S(1)} %fusion.12), kind=kOutput, calls=%fused_computation.18 | convolution fusion | flops 52102784 | bytes 3545088 | tf_op jit(solution)/shard_map/chqk,cqhd->ckhd/dot_general | solution.py:263
  166.0 1.5 copy.47
  167.5 1.1 copy.114
  168.6 0.0 all-gather.8.cloned.1.call-update
  168.6 2.7 %fusion.17 = bf16[4,64,6,128]{3,1,2,0:T(8,128)(2,1)S(1)} fusion(bf16[4,128,6,128]{3,2,1,0:T(8,128)(2,1)S(1)} %reshape.93, f32[4,6,64]{2,1,0:T(8,128)S(1)} %get-tuple-element.6, f32[4,6,64,128]{3,2,1,0:T(8,128)S(1)} %fusion.12), kind=kOutput, calls=%fused_computation.30 | convolution fusion | flops 51119744 | bytes 1972224 | tf_op jit(solution)/shard_map/chqk,ckhd->cqhd/dot_general | solution.py:253
  171.3 0.3 copy.40
  171.6 0.3 fusion.16
  172.0 0.0 copy-start.6
  172.0 0.3 copy.44
  172.3 1.0 copy_bitcast_fusion.3
  173.3 28.9 %all-gather.8.cloned.1.call-done = bf16[512,1536]{0,1:T(8,128)(2,1)} async-done(((bf16[512,768]{0,1:T(8,128)(2,1)}), bf16[512,1536]{0,1:T(8,128)(2,1)}) %all-gather.8.cloned.1.call-update) | async-done | bytes 1572880 | tf_op jit(solution)/shard_map/all_gather | solution.py:265
  202.1 2.8 %convolution_convert_fusion = bf16[512,768]{1,0:T(8,128)(2,1)S(1)} fusion(bf16[512,1536]{0,1:T(8,128)(2,1)} %all-gather.8.cloned.1.call-done, bf16[1536,768]{1,0:T(8,128)(2,1)S(1)} %copy-done.6), kind=kOutput, calls=%fused_computation.12 | convolution fusion | flops 1208352768 | bytes 4718592 | tf_op jit(solution)/shard_map/dot_general | solution.py:266
  205.0 0.9 reshape.94
  205.9 2.6 %fusion.18 = bf16[4,64,6,128]{3,1,2,0:T(8,128)(2,1)} fusion(bf16[4,128,6,128]{3,2,1,0:T(8,128)(2,1)S(1)} %reshape.94, f32[4,6,128]{2,1,0:T(8,128)S(1)} %get-tuple-element.4, f32[4,6,128,64]{2,3,1,0:T(8,128)} %copy-done.5), kind=kOutput, calls=%fused_computation.31 | convolution fusion | flops 51121216 | bytes 1978368 | tf_op jit(solution)/shard_map/chqk,cqhd->ckhd/dot_general | solution.py:268
  208.5 1.5 multiply_reduce_fusion.1
  210.0 2.2 fusion.15
  212.2 0.3 copy.52
  212.5 0.3 copy.54
  212.8 1.0 copy_bitcast_fusion.1
  (23 shorter events, 0.1 us)
Async XLA Ops:
  7.2 75.0 %all-gather.4.cloned.1.call-start = ((), (), s32[]{:S(2)}) async-start(), calls=%async_computation.1 | async-start | bytes 2949120 | tf_op jit(solution)/shard_map/all_gather | solution.py:224
  7.9 84.1 %all-gather.6.cloned.1.call-start = ((), (), s32[]{:S(2)}) async-start(), calls=%async_computation.2 | async-start | bytes 2949120 | tf_op jit(solution)/shard_map/all_gather | solution.py:225
  8.6 138.6 %reduce-scatter.2.cloned.1.call-start = ((), (), s32[]{:S(2)}) async-start(), calls=%async_computation.3 | async-start | bytes 4718592 | tf_op jit(solution)/shard_map/reduce_scatter | solution.py:244
  9.6 1.7 copy-start
  11.3 67.8 %copy-start.11 = (bf16[256,768]{1,0:T(8,128)(2,1)S(1)}, bf16[256,768]{1,0:T(8,128)(2,1)}, u32[]{:S(2)}) copy-start(bf16[256,768]{1,0:T(8,128)(2,1)} %param.11) | copy-start | bytes 1179652
  11.3 68.2 %copy-start.12 = (bf16[256,768]{1,0:T(8,128)(2,1)S(1)}, bf16[256,768]{1,0:T(8,128)(2,1)}, u32[]{:S(2)}) copy-start(bf16[256,768]{1,0:T(8,128)(2,1)} %param.12) | copy-start | bytes 1179652
  80.0 9.0 %copy-start.8 = (bf16[4,64,6,128]{3,2,1,0:T(8,128)(2,1)}, bf16[4,64,6,128]{3,2,1,0:T(8,128)(2,1)S(1)}, u32[]{:S(2)}) copy-start(bf16[4,64,6,128]{3,2,1,0:T(8,128)(2,1)S(1)} %reshape.80) | copy-start | bytes 1179652
  80.0 2.2 copy-start.15
  87.1 3.3 %copy-start.3 = (bf16[4,128,6,128]{3,2,1,0:T(8,128)(2,1)}, bf16[4,128,6,128]{3,2,1,0:T(8,128)(2,1)S(1)}, u32[]{:S(2)}) copy-start(bf16[4,128,6,128]{3,2,1,0:T(8,128)(2,1)S(1)} %reshape.92) | copy-start | bytes 2359300
  87.8 2.6 %copy-start.5 = (f32[4,6,128,64]{2,3,1,0:T(8,128)}, f32[4,6,128,64]{2,3,1,0:T(8,128)S(1)}, u32[]{:S(2)}) copy-start(f32[4,6,128,64]{2,3,1,0:T(8,128)S(1)} %convolution_multiply_fusion.3) | copy-start | bytes 2359300
  96.8 1.0 copy-start.13
  96.8 50.5 %copy-start.1 = (f32[512,1536]{1,0:T(8,128)S(1)}, f32[512,1536]{1,0:T(8,128)}, u32[]{:S(2)}) copy-start(f32[512,1536]{1,0:T(8,128)} %bitcast_convert_fusion) | copy-start | bytes 9437188
  96.8 105.3 %all-gather.8.cloned.1.call-start = ((), (), s32[]{:S(2)}) async-start(), calls=%async_computation.4 | async-start | bytes 2359296 | tf_op jit(solution)/shard_map/all_gather | solution.py:265
  149.7 7.9 %copy-start.10 = (bf16[4,64,6,128]{3,2,1,0:T(8,128)(2,1)S(1)}, bf16[4,64,6,128]{3,2,1,0:T(8,128)(2,1)}, u32[]{:S(2)}) copy-start(bf16[4,64,6,128]{3,2,1,0:T(8,128)(2,1)} %reshape.85) | copy-start | bytes 1179652
  157.7 1.3 copy-start.2
  172.0 30.2 %copy-start.6 = (bf16[1536,768]{1,0:T(8,128)(2,1)S(1)}, bf16[1536,768]{1,0:T(8,128)(2,1)}, u32[]{:S(2)}) copy-start(bf16[1536,768]{1,0:T(8,128)(2,1)} %all-gather.6.cloned.1.call-done) | copy-start | bytes 7077892
  205.9 2.6 %copy-start.7 = (f32[4,6,128,64]{2,3,1,0:T(8,128)S(1)}, f32[4,6,128,64]{2,3,1,0:T(8,128)}, u32[]{:S(2)}) copy-start(f32[4,6,128,64]{2,3,1,0:T(8,128)} %get-tuple-element.5) | copy-start | bytes 2359300
  205.9 2.6 %copy-start.9 = (bf16[4,64,6,128]{3,2,1,0:T(8,128)(2,1)S(1)}, bf16[4,64,6,128]{3,2,1,0:T(8,128)(2,1)}, u32[]{:S(2)}) copy-start(bf16[4,64,6,128]{3,2,1,0:T(8,128)(2,1)} %copy-done.8) | copy-start | bytes 1179652
  208.5 1.5 copy-start.4
  210.0 2.5 %copy-start.14 = (bf16[4,64,6,128]{3,1,2,0:T(8,128)(2,1)S(1)}, bf16[4,64,6,128]{3,1,2,0:T(8,128)(2,1)}, u32[]{:S(2)}) copy-start(bf16[4,64,6,128]{3,1,2,0:T(8,128)(2,1)} %fusion.18) | copy-start | bytes 1179652
Sparse Core Ops, SparseCore 0:
  9.8 39.3 all-gather.3
  51.0 36.8 all-gather.5
  96.9 50.2 reduce-scatter.1
  168.8 33.3 all-gather.7

commit v2 on v1

--- a/solution.py
+++ b/solution.py
@@ -190,95 +190,140 @@
     )(req, database)
 
 
-def softmax_rows(scores):
-    top = jnp.max(scores, axis=-1, keepdims=True)
-    weights = jnp.exp(scores - top)
-    return weights / jnp.sum(weights, axis=-1, keepdims=True)
-
-
-def local(
-    queries,
-    ctx_keys,
-    ctx_values,
-    cotangent,
-    owner,
-    slot_row,
-    database,
-    enc_gain,
-    enc_query_w,
-    enc_out_w,
-):
-    half = queries.shape[1]
+def dot(a, b, dims):
+    return lax.dot_general(a, b, (dims, ((), ())), preferred_element_type=jnp.float32)
+
+
+AB = ((1,), (0,))
+ABT = ((1,), (1,))
+ATB = ((0,), (0,))
+
+
+def block_kernel(f_ref, wq_ref, wo_ref, gain_ref, q_ref, k_ref, v_ref, t_ref,
+                 att_ref, gq_ref, gk_ref, gv_ref,
+                 encq, probs, mixed, part_own, part_out, part_in, denc, denc_in, dmix,
+                 p_send, p_recv, d_send, d_recv):
+    m = lax.axis_index("mp")
+    mate = (lax.axis_index("section"), lax.axis_index("shard"), 1 - m)
+    scale = DH ** (-0.5)
+    f32, bf = jnp.float32, jnp.bfloat16
+    heads = q_ref.shape[1] // DH
+    half = heads * DH
+    spans = q_ref.shape[0] // CT
+    rows_n = K * NT
+    own = pl.ds(pl.multiple_of(m * half, 128), half)
+    other = pl.ds(pl.multiple_of((1 - m) * half, 128), half)
+    barrier = pltpu.get_barrier_semaphore()
+    pl.semaphore_signal(barrier, inc=1, device_id=mate, device_id_type=MESH)
+    pl.semaphore_wait(barrier, 1)
+
+    def send(src, dst, ss, rs, g):
+        rows = pl.ds(pl.multiple_of(g * rows_n, rows_n), rows_n)
+        return pltpu.make_async_remote_copy(
+            src.at[rows], dst.at[rows], ss.at[g], rs.at[g], device_id=mate, device_id_type=MESH)
+
+    def encode(g, _):
+        rows = pl.ds(pl.multiple_of(g * rows_n, rows_n), rows_n)
+        toks = pl.ds(pl.multiple_of(g * CT, CT), CT)
+        wide = f_ref[rows, :].astype(f32)
+        mean = jnp.mean(wide * wide, axis=1, keepdims=True)
+        normed = (wide * lax.rsqrt(mean + 1e-06) * gain_ref[...]).astype(bf)
+        encq[rows, :] = dot(normed, wq_ref[...], AB).astype(bf)
+        for h in range(heads):
+            cols = slice(h * DH, (h + 1) * DH)
+            st = dot(k_ref[toks, cols], encq[rows, cols], ABT) * scale
+            e = jnp.exp(st - jnp.max(st, axis=0, keepdims=True))
+            p = e / jnp.sum(e, axis=0, keepdims=True)
+            probs[g * heads + h] = p
+            mixed[:, cols] = dot(p.astype(bf), v_ref[toks, cols], ATB).astype(bf)
+        part_out[rows, :] = dot(mixed[...], wo_ref[other, :], ABT).astype(bf)
+        send(part_out, part_in, p_send, p_recv, g).start()
+        part_own[rows, :] = dot(mixed[...], wo_ref[own, :], ABT)
+        return 0
+
+    def cross(g, _):
+        rows = pl.ds(pl.multiple_of(g * rows_n, rows_n), rows_n)
+        toks = pl.ds(pl.multiple_of(g * CT, CT), CT)
+        send(part_out, part_in, p_send, p_recv, g).wait()
+        for h in range(heads):
+            cols = slice(h * DH, (h + 1) * DH)
+            raw = f_ref[rows, pl.ds(pl.multiple_of(m * half + h * DH, 128), DH)].astype(f32)
+            enc = (raw + (part_own[rows, cols] + part_in[rows, cols].astype(f32))).astype(bf)
+            q, t = q_ref[toks, cols], t_ref[toks, cols]
+            both = dot(jnp.concatenate([q, t], axis=0), enc, ABT)
+            s, dp = both[:CT] * scale, both[CT:]
+            e = jnp.exp(s - jnp.max(s, axis=1, keepdims=True))
+            p = e / jnp.sum(e, axis=1, keepdims=True)
+            pb = p.astype(bf)
+            ds = (p * (dp - jnp.sum(dp * p, axis=1, keepdims=True))).astype(bf)
+            out = dot(jnp.concatenate([pb, ds], axis=0), enc, AB)
+            att_ref[toks, cols] = out[:CT].astype(bf)
+            gq_ref[toks, cols] = (scale * out[CT:]).astype(bf)
+            denc[rows, cols] = (scale * dot(ds, q, ATB) + dot(pb, t, ATB)).astype(bf)
+        send(denc, denc_in, d_send, d_recv, g).start()
+        return 0
+
+    def back(g, _):
+        rows = pl.ds(pl.multiple_of(g * rows_n, rows_n), rows_n)
+        toks = pl.ds(pl.multiple_of(g * CT, CT), CT)
+        near = dot(denc[rows, :], wo_ref[own, :], AB)
+        send(denc, denc_in, d_send, d_recv, g).wait()
+        dmix[...] = (near + dot(denc_in[rows, :], wo_ref[other, :], AB)).astype(bf)
+        for h in range(heads):
+            cols = slice(h * DH, (h + 1) * DH)
+            p = probs[g * heads + h]
+            dm = dmix[:, cols]
+            gv_ref[toks, cols] = dot(p.astype(bf), dm, AB).astype(bf)
+            dpe = dot(v_ref[toks, cols], dm, ABT)
+            dse = (p * (dpe - jnp.sum(dpe * p, axis=0, keepdims=True))).astype(bf)
+            gk_ref[toks, cols] = (scale * dot(dse, encq[rows, cols], AB)).astype(bf)
+        return 0
+
+    lax.fori_loop(0, spans, encode, 0)
+    lax.fori_loop(0, spans, cross, 0)
+    lax.fori_loop(0, spans, back, 0)
+
+
+def blocks_pass(fetched, wq, wo, gain, queries, keys, values, cotangent):
+    dma = pltpu.SemaphoreType.DMA
+    bf, f32 = jnp.bfloat16, jnp.float32
+    tokens, half = queries.shape
+    spans, heads = tokens // CT, half // DH
+    rows = spans * K * NT
+    out = jax.ShapeDtypeStruct((tokens, half), bf)
+    vmem = pl.BlockSpec(memory_space=pltpu.VMEM)
+    return pl.pallas_call(
+        block_kernel,
+        out_shape=(out,) * 4,
+        in_specs=[vmem] * 8,
+        out_specs=(vmem,) * 4,
+        scratch_shapes=[
+            pltpu.VMEM((rows, half), bf),
+            pltpu.VMEM((spans * heads, CT, K * NT), f32),
+            pltpu.VMEM((K * NT, half), bf),
+            pltpu.VMEM((rows, half), f32),
+            pltpu.VMEM((rows, half), bf),
+            pltpu.VMEM((rows, half), bf),
+            pltpu.VMEM((rows, half), bf),
+            pltpu.VMEM((rows, half), bf),
+            pltpu.VMEM((K * NT, half), bf),
+            dma((spans,)), dma((spans,)), dma((spans,)), dma((spans,)),
+        ],
+        compiler_params=pltpu.CompilerParams(
+            collective_id=1, has_side_effects=True, vmem_limit_bytes=40 * 1024 * 1024),
+        cost_estimate=pl.CostEstimate(flops=4_600_000_000, bytes_accessed=12_000_000, transcendentals=600_000),
+    )(fetched, wq, wo, gain, queries, keys, values, cotangent)
+
+
+def local(queries, ctx_keys, ctx_values, cotangent, owner, slot_row, database, enc_gain, enc_query_w, enc_out_w):
     width = database.shape[2]
-    heads = half // DH
-    blocks = owner.shape[0]
-    scale = DH ** (-0.5)
-    part = lax.axis_index("mp")
     wanted = (owner * database.shape[0] + slot_row).reshape(1, -1)
     request = jnp.pad(wanted, ((0, 7), (0, 128 - wanted.shape[1])))
-    fetched = fetch(request, database)
-    wide = fetched.reshape(-1, width).astype(jnp.float32)
-    squares = jnp.mean(wide * wide, axis=1, keepdims=True)
-    normed = (wide * lax.rsqrt(squares + 1e-06) * enc_gain).astype(jnp.bfloat16)
-    query_full, out_full = (
-        lax.all_gather(enc_query_w, "section", axis=0, tiled=True),
-        lax.all_gather(enc_out_w, "section", axis=0, tiled=True),
-    )
-    enc_q = jnp.dot(normed, query_full, preferred_element_type=jnp.float32).astype(jnp.bfloat16)
-    enc_q4 = enc_q.reshape(blocks, K * NT, heads, DH)
-    keys4 = ctx_keys.reshape(blocks, CT, heads, DH)
-    values4 = ctx_values.reshape(blocks, CT, heads, DH)
-    enc_p = softmax_rows(
-        jnp.einsum("cqhd,ckhd->chqk", enc_q4, keys4, preferred_element_type=jnp.float32) * scale
-    )
-    enc_pb = enc_p.astype(jnp.bfloat16)
-    mixed = jnp.einsum(
-        "chqk,ckhd->cqhd", enc_pb, values4, preferred_element_type=jnp.float32
-    ).astype(jnp.bfloat16)
-    projected = lax.dot_general(
-        mixed.reshape(-1, half),
-        out_full,
-        (((1,), (1,)), ((), ())),
-        preferred_element_type=jnp.float32,
-    )
-    own_sum = lax.psum_scatter(projected, "mp", scatter_dimension=1, tiled=True)
-    residual = lax.dynamic_slice_in_dim(wide, part * half, half, 1)
-    encoded = (residual + own_sum).astype(jnp.bfloat16)
-    enc4 = encoded.reshape(blocks, K * NT, heads, DH)
-    query4 = queries.reshape(blocks, CT, heads, DH)
-    cca_p = softmax_rows(
-        jnp.einsum("cqhd,ckhd->chqk", query4, enc4, preferred_element_type=jnp.float32) * scale
-    )
-    cca_pb = cca_p.astype(jnp.bfloat16)
-    attended = jnp.einsum(
-        "chqk,ckhd->cqhd", cca_pb, enc4, preferred_element_type=jnp.float32
-    ).astype(jnp.bfloat16)
-    grad4 = cotangent.reshape(blocks, CT, heads, DH)
-    d_p = jnp.einsum("cqhd,ckhd->chqk", grad4, enc4, preferred_element_type=jnp.float32)
-    d_s = (cca_p * (d_p - jnp.sum(d_p * cca_p, axis=-1, keepdims=True))).astype(jnp.bfloat16)
-    grad_queries = (
-        scale * jnp.einsum("chqk,ckhd->cqhd", d_s, enc4, preferred_element_type=jnp.float32)
-    ).astype(jnp.bfloat16)
-    key_part = jnp.einsum("chqk,cqhd->ckhd", d_s, query4, preferred_element_type=jnp.float32)
-    value_part = jnp.einsum("chqk,cqhd->ckhd", cca_pb, grad4, preferred_element_type=jnp.float32)
-    d_enc = (scale * key_part + value_part).astype(jnp.bfloat16)
-    d_full = lax.all_gather(d_enc.reshape(-1, half), "mp", axis=1, tiled=True)
-    d_mixed = jnp.dot(d_full, out_full, preferred_element_type=jnp.float32).astype(jnp.bfloat16)
-    d_mixed4 = d_mixed.reshape(blocks, K * NT, heads, DH)
-    grad_values = jnp.einsum(
-        "chqk,cqhd->ckhd", enc_pb, d_mixed4, preferred_element_type=jnp.float32
-    ).astype(jnp.bfloat16)
-    d_pe = jnp.einsum("cqhd,ckhd->chqk", d_mixed4, values4, preferred_element_type=jnp.float32)
-    d_se = (enc_p * (d_pe - jnp.sum(d_pe * enc_p, axis=-1, keepdims=True))).astype(jnp.bfloat16)
-    grad_keys = (
-        scale * jnp.einsum("chqk,cqhd->ckhd", d_se, enc_q4, preferred_element_type=jnp.float32)
-    ).astype(jnp.bfloat16)
-    shape = (blocks * CT, half)
-    return (
-        attended.reshape(shape),
-        grad_queries.reshape(shape),
-        grad_keys.reshape(shape),
-        grad_values.reshape(shape),
+    fetched = fetch(request, database).reshape(-1, width)
+    query_full = lax.all_gather(enc_query_w, "section", axis=0, tiled=True)
+    out_full = lax.all_gather(enc_out_w, "section", axis=0, tiled=True)
+    return blocks_pass(
+        fetched, query_full, out_full, enc_gain.reshape(1, -1), queries, ctx_keys, ctx_values, cotangent
     )
 
 

time: 221 us -> 142 us (0.64)
  waiting for transfers between devices: 76.2 us -> 9.67 us
  Pallas kernels: 67.3 us -> 108 us
  matrix products: 32.6 us -> 0 us
  other arithmetic: 11.6 us -> 0.7 us
  local copies, waits for them, and re-layouts: 18.2 us -> 8.87 us
    reduce_scatter x1 -> x0, waiting for transfers between devices: 46 us -> none  [local(): own_sum = lax.psum_scatter(projected, 'mp', scatter_dimension=1, tiled=True)]
    pallas_call x0 -> x1, Pallas kernels: none -> 40.6 us  [blocks_pass(): pl.pallas_call(block_kernel, out_shape=(out,) * 4, in_specs=[vmem] * 8, o...]
    dot_general x14 -> x0, matrix products: 32.6 us -> none  [the longest x1 5.47 us: local(): jnp.einsum('chqk,cqhd->ckhd', cca_pb, grad4, preferred_element_type=jnp.f...]
    all_gather x3 -> x2, waiting for transfers between devices: 28.9 us -> 8.32 us  [the longest x1 8.3 us: local(): out_full = lax.all_gather(enc_out_w, 'section', axis=0, tiled=True)]
    reshape x9 -> x1, local copies, waits for them, and re-layouts: 10.2 us -> 0.7 us  [local(): enc_gain.reshape(1, -1)]
    sub x2 -> x0, other arithmetic: 5.39 us -> none  [softmax_rows(): weights = jnp.exp(scores - top)]
    convert_element_type x3 -> x0, other arithmetic: 5.11 us -> none  [the longest x1 2.45 us: local(): encoded = (residual + own_sum).astype(jnp.bfloat16)]
    unnamed x33 -> x18, local copies, waits for them, and re-layouts: 3.56 us -> 7.98 us
  transfers between devices with their start and end apart: 4 -> 2, of which waited for: 2 -> 1; matrix products, arithmetic and copies ran while one was open for 10% -> 1% of each run, Pallas kernels for 31% -> 48%
where the time goes in v2:
time: 142 us; the launch traced here: 141 us
  Pallas kernels  108 us (76%)
  between operations  14.1 us (10%)
  waiting for transfers between devices  9.67 us (7%)
  local copies, waits for them, and re-layouts  8.87 us (6%)
    pallas_call x1, Pallas kernels, fetch(): pl.pallas_call(fetch_kernel, out_shape=jax.ShapeDtypeStruct((8, 64, 1536)...  67.3 us
    pallas_call x1, Pallas kernels, blocks_pass(): pl.pallas_call(block_kernel, out_shape=(out,) * 4, in_specs=[vmem] * 8, o...  40.6 us
    all_gather x1, waiting for transfers between devices, local(): out_full = lax.all_gather(enc_out_w, 'section', axis=0, tiled=True)  8.3 us
    unnamed x18, local copies, waits for them, and re-layouts  7.98 us
  transfers between devices with their start and end apart: 2, of which 1 were waited for; matrix products, arithmetic and copies ran while one was open for 1% of the time, Pallas kernels for 48%

profile of v2, /device:TPU:1, one launch (start us, length us, event | category | flops | bytes accessed | tf_op | source)
XLA Modules:
  0.0 141.3 jit_solution(13744050239021916216)
XLA Ops:
  7.2 0.0 all-gather.3.cloned.1.call-start
  7.2 0.0 copy-start.4
  7.2 0.0 copy-start.5
  7.2 0.7 all-gather.3.cloned.1.call-update
  7.9 0.0 copy-start.3
  7.9 0.0 all-gather.5.cloned.1.call-start
  8.0 0.7 all-gather.5.cloned.1.call-update
  8.7 0.7 multiply_add_fusion
  9.4 0.1 copy.15
  9.5 0.1 reshape.17
  9.5 0.7 reshape.19.gain_ref
  10.3 0.0 copy-start
  10.3 1.7 %copy-done = bf16[12,64,1536]{2,1,0:T(8,128)(2,1)S(1)} copy-done((bf16[12,64,1536]{2,1,0:T(8,128)(2,1)S(1)}, bf16[12,64,1536]{2,1,0:T(8,128)(2,1)}, u32[]{:S(2)}) %copy-start) | copy-done | bytes 2359320
  11.9 0.0 copy-start.6
  11.9 67.3 %shard_map.129 = bf16[8,64,1536]{2,1,0:T(8,128)(2,1)S(1)} custom-call(s32[8,128]{1,0:T(8,128)S(1)} %pad.4.req_ref, bf16[12,64,1536]{2,1,0:T(8,128)(2,1)S(1)} %copy-done), custom_call_target="tpu_custom_call" | custom-call | bytes 12000000 | tf_op jit(solution)/shard_map/pallas_call | solution.py:170
  79.2 0.0 all-gather.3.cloned.1.call-done.wq_ref
  79.2 8.3 %all-gather.5.cloned.1.call-done.wo_ref = bf16[1536,768]{1,0:T(8,128)(2,1)} async-done(((bf16[384,768]{1,0:T(8,128)(2,1)}), bf16[1536,768]{1,0:T(8,128)(2,1)}) %all-gather.5.cloned.1.call-update) | async-done | bytes 2359312 | tf_op jit(solution)/shard_map/all_gather | solution.py:324
  87.5 0.0 copy-done.4
  87.5 0.0 copy-done.5
  87.5 0.0 copy-done.3
  87.5 0.0 copy-done.6
  87.6 0.0 copy-start.1
  87.6 1.7 %copy-done.1 = bf16[1536,768]{1,0:T(8,128)(2,1)S(1)} copy-done((bf16[1536,768]{1,0:T(8,128)(2,1)S(1)}, bf16[1536,768]{1,0:T(8,128)(2,1)}, u32[]{:S(2)}) %copy-start.1) | copy-done | bytes 2359320
  89.2 0.0 copy-start.2
  89.2 1.7 %copy-done.2 = bf16[1536,768]{1,0:T(8,128)(2,1)S(1)} copy-done((bf16[1536,768]{1,0:T(8,128)(2,1)S(1)}, bf16[1536,768]{1,0:T(8,128)(2,1)}, u32[]{:S(2)}) %copy-start.2) | copy-done | bytes 2359320
  90.9 40.6 %shard_map.130 = (bf16[256,768]{1,0:T(8,128)(2,1)S(1)}, bf16[256,768]{1,0:T(8,128)(2,1)S(1)}, bf16[256,768]{1,0:T(8,128)(2,1)S(1)}, bf16[256,768]{1,0:T(8,128)(2,1)S(1)}) custom-call(bf16[512,1536]{1,0:T(8,128)(2,1)S(1)} %bitcast.1, bf16[1536,768]{1,0:T(8,128)(2,1)S(1)} %copy-done.1, bf16[1536,768]{1,0:T(8,128)(2,1)S(1)} %copy-done.2, ...), custom_call_target="tpu_custom_call" | custom-call | flops 4600000000 | bytes 12000000 | tf_op jit(solution)/shard_map/pallas_call | solution.py:295
  131.5 0.7 copy.20
  132.2 0.7 copy.21
  133.0 0.7 copy.22
  133.7 0.7 copy.23
  (1 shorter events, 0.0 us)
Async XLA Ops:
  7.2 72.1 %all-gather.3.cloned.1.call-start = ((), (), s32[]{:S(2)}) async-start(), calls=%async_computation | async-start | bytes 2949120 | tf_op jit(solution)/shard_map/all_gather | solution.py:323
  7.2 80.3 %copy-start.4 = (bf16[256,768]{1,0:T(8,128)(2,1)S(1)}, bf16[256,768]{1,0:T(8,128)(2,1)}, u32[]{:S(2)}) copy-start(bf16[256,768]{1,0:T(8,128)(2,1)} %k_ref.1) | copy-start | bytes 1179652
  7.2 80.3 %copy-start.5 = (bf16[256,768]{1,0:T(8,128)(2,1)S(1)}, bf16[256,768]{1,0:T(8,128)(2,1)}, u32[]{:S(2)}) copy-start(bf16[256,768]{1,0:T(8,128)(2,1)} %v_ref.1) | copy-start | bytes 1179652
  7.9 79.6 %copy-start.3 = (bf16[256,768]{1,0:T(8,128)(2,1)S(1)}, bf16[256,768]{1,0:T(8,128)(2,1)}, u32[]{:S(2)}) copy-start(bf16[256,768]{1,0:T(8,128)(2,1)} %q_ref.1) | copy-start | bytes 1179652
  7.9 79.6 %all-gather.5.cloned.1.call-start = ((), (), s32[]{:S(2)}) async-start(), calls=%async_computation.1 | async-start | bytes 2949120 | tf_op jit(solution)/shard_map/all_gather | solution.py:324
  10.3 1.7 %copy-start = (bf16[12,64,1536]{2,1,0:T(8,128)(2,1)S(1)}, bf16[12,64,1536]{2,1,0:T(8,128)(2,1)}, u32[]{:S(2)}) copy-start(bf16[12,64,1536]{2,1,0:T(8,128)(2,1)} %db_ref.1) | copy-start | bytes 7077892
  11.9 75.6 %copy-start.6 = (bf16[256,768]{1,0:T(8,128)(2,1)S(1)}, bf16[256,768]{1,0:T(8,128)(2,1)}, u32[]{:S(2)}) copy-start(bf16[256,768]{1,0:T(8,128)(2,1)} %t_ref.1) | copy-start | bytes 1179652
  87.6 1.7 %copy-start.1 = (bf16[1536,768]{1,0:T(8,128)(2,1)S(1)}, bf16[1536,768]{1,0:T(8,128)(2,1)}, u32[]{:S(2)}) copy-start(bf16[1536,768]{1,0:T(8,128)(2,1)} %all-gather.3.cloned.1.call-done.wq_ref) | copy-start | bytes 7077892
  89.2 1.7 %copy-start.2 = (bf16[1536,768]{1,0:T(8,128)(2,1)S(1)}, bf16[1536,768]{1,0:T(8,128)(2,1)}, u32[]{:S(2)}) copy-start(bf16[1536,768]{1,0:T(8,128)(2,1)} %all-gather.5.cloned.1.call-done.wo_ref) | copy-start | bytes 7077892
Sparse Core Ops, SparseCore 0:
  9.8 39.3 all-gather.2
  51.0 36.4 all-gather.4

commit v3 on v0

v3 whole, which is shorter than its diff:
```python
import jax
import jax.numpy as jnp
from jax import lax
from jax.experimental import pallas as pl
from jax.experimental.pallas import tpu as pltpu
from jax.sharding import PartitionSpec as P

DH = 128
CT = 64
NT = 64
K = 2
DB = 12
SPANS = 4
REQ = SPANS * K
TOK = NT // 4
COL = 16 * DB
ROWS = K * NT
MESH = pl.DeviceIdType.MESH
AB = ((1,), (0,))
ABT = ((1,), (1,))
ATB = ((0,), (0,))
ORDER = [(ds, dc) for ds in (2, 1, 3, 0) for dc in (0, 1)]
PEERS = [p for p in ORDER if p != (0, 0)]
A, B = 0, 1
LAG = 3
ZLIST = sorted([(k + LAG * grp, grp, k) for grp in (A, B) for k in range(4)])


def dot(a, b, dims):
    return lax.dot_general(a, b, (dims, ((), ())), preferred_element_type=jnp.float32)


def place(t):
    return (t // 3) * 2 + t % 3 if t % 3 < 2 else 4 + t // 3


def al(v, n):
    return pl.multiple_of(v, n)


def kernel(owner_hbm, row_hbm, db_ref, gain_ref, wq_hbm, wo_hbm, q_hbm, k_hbm, v_hbm, t_hbm,
           att_hbm, gq_hbm, gk_hbm, gv_hbm,
           att_ref, gq_ref, gk_ref, gv_ref, who, row, req, rq, rqs, gath_a, gath_b, xs, xr, xm_a, xm_b, f_ref, wq_ref, wo_ref, q_ref, k_ref, v_ref, t_ref,
           normed, encq, probs, mixed, part_own, part_out, part_in, denc, denc_in, dmix,
           loc, rq_send, rq_recv, rx_send, rx_recv, sib_send, sib_recv, px_send, px_recv,
           zp_send, zp_recv, zm_send, zm_recv, x_send, x_recv, y_send, y_recv, m_send, m_recv,
           wy_send, wy_recv, ws_send, ws_recv, p_send, p_recv, d_send, d_recv, out_sem):
    s = lax.axis_index("section")
    d = lax.axis_index("shard")
    m = lax.axis_index("mp")
    x, z, c = d // 16, (d // 2) % 8, d % 2
    f32, bf = jnp.float32, jnp.bfloat16

    def dev(s_, x_, z_, c_, m_):
        return (s_, x_ * 16 + z_ * 2 + c_, m_)

    def peer(ds, dc):
        return dev((s + ds) % 4, x, z, (c + dc) % 2, m)

    pair = dev(s, 1 - x, z, c, m)
    up, down = dev(s, x, (z + 1) % 8, c, m), dev(s, x, (z + 7) % 8, c, m)
    mate = dev(s, x, z, c, 1 - m)
    sib = dev(s, x, z, 1 - c, m)
    me = s * 2 + c

    def remote(src, dst, ss, rs, to):
        return pltpu.make_async_remote_copy(src, dst, ss, rs, device_id=to, device_id_type=MESH)

    friends = [peer(*p) for p in PEERS] + [pair, up, down, mate]
    barrier = pltpu.get_barrier_semaphore()
    for f in friends:
        pl.semaphore_signal(barrier, inc=1, device_id=f, device_id_type=MESH)

    tok = pl.ds(al(s * TOK, TOK), TOK)

    def feat(core, ch):
        return pl.ds(al(((2 * m + core) * 3 + ch) * 128, 128), 128)

    def slot(ch, place):
        if ch < 2:
            return gath_a.at[pl.ds(place, DB), ch]
        return gath_b.at[x, pl.ds(place, DB)]

    here = z * 24 + c * DB
    small = [pltpu.make_async_copy(owner_hbm, who, loc.at[9]), pltpu.make_async_copy(row_hbm, row, loc.at[10])]
    for cp in small:
        cp.start()
    mine, to_sib = [], []
    for ch in range(3):
        cp = pltpu.make_async_copy(db_ref.at[:, tok, feat(c, ch)], slot(ch, here), loc.at[ch])
        cp.start()
        mine.append(cp)
    pl.semaphore_wait(barrier, len(friends))
    for ch in range(3):
        cp = remote(db_ref.at[:, tok, feat(1 - c, ch)], slot(ch, here), sib_send.at[ch], sib_recv.at[ch], sib)
        cp.start()
        to_sib.append(cp)
    to_pair = []
    for h in range(2):
        part = gath_b.at[x, pl.ds(z * 24 + ((c + h) % 2) * DB, DB)]
        to_pair.append(remote(part, part, px_send.at[h], px_recv.at[h], pair))
    lane = lax.broadcasted_iota(jnp.int32, (8, 128), 1)
    wanted = jnp.zeros((8, 128), jnp.int32)
    for cp in small:
        cp.wait()
    for j in range(REQ):
        g = who[j % K, j // K] * DB + row[j % K, j // K]
        wanted = jnp.where(lane == j, g, wanted)
    req[...] = wanted
    rq[x * 8 + me] = wanted
    rq_copies = []
    for i, p in enumerate(PEERS):
        cp = remote(req, rq.at[x * 8 + me], rq_send.at[i], rq_recv.at[i], peer(*p))
        cp.start()
        rq_copies.append(cp)

    plus, minus = {}, {}

    def zcopy(grp, k, h, up_way):
        zz = (z + 8 - k) % 8 if up_way else (z + k) % 8
        blocks = pl.ds(zz * 24 + ((c + h) % 2) * DB, DB)
        sl = gath_a.at[blocks] if grp == A else gath_b.at[:, blocks]
        i = grp * 7 + k * 2 + (h if k < 3 else 0)
        if up_way:
            return remote(sl, sl, zp_send.at[i], zp_recv.at[i], up)
        return remote(sl, sl, zm_send.at[i], zm_recv.at[i], down)

    def zstep(grp, k):
        for h in range(2):
            if k == 0:
                if grp == B:
                    to_pair[h].wait_recv()
                elif h == 0:
                    mine[0].wait()
                    mine[1].wait()
                else:
                    to_sib[0].wait_recv()
                    to_sib[1].wait_recv()
            ways = (True, False) if k < 3 else ((True,) if h == 0 else (False,))
            for way in ways:
                done = plus if way else minus
                if k:
                    done[grp, k - 1, h].wait_recv()
                cp = zcopy(grp, k, h, way)
                cp.start()
                done[grp, k, h] = cp

    def zdone(grp):
        plus[grp, 2, 1].wait_recv()
        minus[grp, 2, 0].wait_recv()
        plus[grp, 3, 0].wait_recv()
        minus[grp, 3, 1].wait_recv()

    def pair_out():
        mine[2].wait()
        to_pair[0].start()
        to_sib[2].wait_recv()
        to_pair[1].start()

    wy, ws, loads = [], [], []

    def weights_out():
        for w, (src, dst) in enumerate(((wq_hbm, wq_ref), (wo_hbm, wo_ref))):
            cp = pltpu.make_async_copy(src, dst.at[pl.ds(al(s * 384, 384), 384)], loc.at[3 + w])
            cp.start()
            loads.append(cp)
            for ds in (2, 1, 3):
                i = w * 3 + ds - 1
                cp = remote(src.at[pl.ds(al(c * 192, 192), 192)],
                            dst.at[pl.ds(al(s * 384 + c * 192, 192), 192)],
                            wy_send.at[i], wy_recv.at[i], peer(ds, 0))
                cp.start()
                wy.append((w, ds, cp))
        for i, (src, dst) in enumerate(((q_hbm, q_ref), (k_hbm, k_ref), (v_hbm, v_ref), (t_hbm, t_ref))):
            cp = pltpu.make_async_copy(src, dst, loc.at[5 + i])
            cp.start()
            loads.append(cp)

    def weights_on():
        for w, ds, cp in wy:
            cp.wait_recv()
            dst = (wq_ref, wo_ref)[w]
            part = dst.at[pl.ds(al(((s + 4 - ds) % 4) * 384 + c * 192, 192), 192)]
            i = w * 3 + ds - 1
            on = remote(part, part, ws_send.at[i], ws_recv.at[i], sib)
            on.start()
            ws.append(on)

    fwd = remote(rq.at[pl.ds(x * 8, 8)], rq.at[pl.ds(x * 8, 8)], rx_send.at[0], rx_recv.at[0], pair)

    def requests_on():
        for cp in rq_copies:
            cp.wait_recv()
        fwd.start()

    def requests_in():
        fwd.wait_recv()
        cp = pltpu.make_async_copy(rq, rqs, loc.at[11])
        cp.start()
        cp.wait()

    xcopies, ycopies, mcopies = {}, {}, []

    def target(i):
        ds, dc = ORDER[i]
        return ((s + ds) % 4) * 2 + (c + dc) % 2

    def select():
        for half in range(2):
            for i in range(half * 4, half * 4 + 4):
                for j in range(REQ):
                    g = rqs[(1 - x) * 8 + target(i), 0, j]
                    xs[i * 8 + j] = gath_a[lax.rem(g, COL)]
            part = pl.ds(half * 32, 32)
            cp = remote(xs.at[part], xr.at[part], x_send.at[half], x_recv.at[half], pair)
            cp.start()
            xcopies[half] = cp

    def deliver(grp, i):
        if grp == A:
            src, dst = xm_a.at[i], f_ref.at[pl.ds(m * 6 + c * 2, 2), :, pl.ds(al(s * 32, 32), 32), :]
        else:
            src, dst = xm_b.at[i], f_ref.at[m * 6 + 4 + c, :, pl.ds(al(s * 32, 32), 32), :]
        n = grp * 8 + i
        if ORDER[i] == (0, 0):
            cp = pltpu.make_async_copy(src, dst, y_recv.at[n])
        else:
            cp = remote(src, dst, y_send.at[n], y_recv.at[n], peer(*ORDER[i]))
        cp.start()
        ycopies[grp, i] = cp

    def merge_a(half):
        xcopies[half].wait_recv()
        for i in range(half * 4, half * 4 + 4):
            for j in range(REQ):
                g = rqs[x * 8 + target(i), 0, j]
                got = jnp.where((g // COL) == x, gath_a[lax.rem(g, COL)], xr[i * 8 + j])
                for ch in range(2):
                    xm_a[i, ch, j // K, (j % K) * TOK:(j % K + 1) * TOK] = got[ch]
            deliver(A, i)

    def merge_b():
        for i in range(8):
            for j in range(REQ):
                g = rqs[x * 8 + target(i), 0, j]
                xm_b[i, j // K, (j % K) * TOK:(j % K + 1) * TOK] = gath_b[g // COL, lax.rem(g, COL)]
            deliver(B, i)

    def arrived(grp, i):
        if ORDER[i] == (0, 0):
            ycopies[grp, i].wait()
        else:
            ycopies[grp, i].wait_recv()

    def onward(part, n):
        cp = remote(part, part, m_send.at[n], m_recv.at[n], mate)
        cp.start()
        mcopies.append(cp)

    def piece_a(i):
        ds, dc = ORDER[i]
        return f_ref.at[pl.ds(m * 6 + ((c + dc) % 2) * 2, 2), :, pl.ds(al(((s + 4 - ds) % 4) * 32, 32), 32), :]

    def piece_b(g):
        return f_ref.at[pl.ds(m * 6 + 4, 2), g]

    def onward_a(half):
        for i in range(half * 4, half * 4 + 4):
            arrived(A, i)
            onward(piece_a(i), i)

    def onward_b():
        for i in range(8):
            arrived(B, i)
        for g in range(SPANS):
            onward(piece_b(g), 8 + g)

    after = {
        (A, 0): [pair_out, weights_out],
        (A, 1): [requests_on],
        (A, 2): [requests_in],
        (B, 0): [lambda: zdone(A), select],
        (B, 2): [lambda: merge_a(0)],
        (B, 3): [lambda: merge_a(1), lambda: onward_a(0), lambda: onward_a(1), lambda: zdone(B), merge_b, weights_on,
                 onward_b],
    }
    for _, grp, k in ZLIST:
        zstep(grp, k)
        for act in after.get((grp, k), []):
            act()
    for i in range(8):
        remote(piece_a(i), piece_a(i), m_send.at[i], m_recv.at[i], mate).wait_recv()
    for cp in ws:
        cp.wait_recv()
    for cp in loads:
        cp.wait()

    scale = DH ** (-0.5)
    heads = q_ref.shape[1] // DH
    width = heads * DH
    own = pl.ds(al(m * width, 128), width)
    other = pl.ds(al((1 - m) * width, 128), width)

    def send(src, dst, ss, rs, g):
        rows = pl.ds(al(g * ROWS, ROWS), ROWS)
        return remote(src.at[rows], dst.at[rows], ss.at[g], rs.at[g], mate)

    outs = ((att_ref, att_hbm), (gq_ref, gq_hbm), (gk_ref, gk_hbm), (gv_ref, gv_hbm))

    def store(n, g):
        toks = pl.ds(al(g * CT, CT), CT)
        return pltpu.make_async_copy(outs[n][0].at[toks], outs[n][1].at[toks], out_sem.at[n, g])

    def encode(g, _):
        rows = pl.ds(al(g * ROWS, ROWS), ROWS)
        toks = pl.ds(al(g * CT, CT), CT)
        remote(piece_b(g), piece_b(g), m_send.at[8 + g], m_recv.at[8 + g], mate).wait_recv()
        squares = jnp.zeros((ROWS, 128), f32)
        for f in range(12):
            tile = f_ref[f, g].astype(f32)
            squares = squares + tile * tile
        mean = jnp.sum(squares, axis=1, keepdims=True) / (2 * width)
        inv = lax.rsqrt(mean + 1e-06)
        for t in range(12):
            f = (t // 6) * 6 + place(t % 6)
            gain = gain_ref[pl.ds(t * 128, 128)].reshape(1, 128)
            normed[:, t * 128:(t + 1) * 128] = (f_ref[f, g].astype(f32) * inv * gain).astype(bf)
        encq[rows, :] = dot(normed[...], wq_ref[...], AB).astype(bf)
        for h in range(heads):
            cols = slice(h * DH, (h + 1) * DH)
            st = dot(k_ref[toks, cols], encq[rows, cols], ABT) * scale
            e = jnp.exp(st - jnp.max(st, axis=0, keepdims=True))
            p = e / jnp.sum(e, axis=0, keepdims=True)
            probs[g * heads + h] = p
            mixed[:, cols] = dot(p.astype(bf), v_ref[toks, cols], ATB).astype(bf)
        part_out[rows, :] = dot(mixed[...], wo_ref[other, :], ABT).astype(bf)
        send(part_out, part_in, p_send, p_recv, g).start()
        part_own[rows, :] = dot(mixed[...], wo_ref[own, :], ABT)
        return 0

    def cross(g, _):
        rows = pl.ds(al(g * ROWS, ROWS), ROWS)
        toks = pl.ds(al(g * CT, CT), CT)
        send(part_out, part_in, p_send, p_recv, g).wait()
        for h in range(heads):
            cols = slice(h * DH, (h + 1) * DH)
            raw = f_ref[m * 6 + place(h), g].astype(f32)
            enc = (raw + (part_own[rows, cols] + part_in[rows, cols].astype(f32))).astype(bf)
            q, t = q_ref[toks, cols], t_ref[toks, cols]
            both = dot(jnp.concatenate([q, t], axis=0), enc, ABT)
            sc, dp = both[:CT] * scale, both[CT:]
            e = jnp.exp(sc - jnp.max(sc, axis=1, keepdims=True))
            p = e / jnp.sum(e, axis=1, keepdims=True)
            pb = p.astype(bf)
            dsc = (p * (dp - jnp.sum(dp * p, axis=1, keepdims=True))).astype(bf)
            out = dot(jnp.concatenate([pb, dsc], axis=0), enc, AB)
            att_ref[toks, cols] = out[:CT].astype(bf)
            gq_ref[toks, cols] = (scale * out[CT:]).astype(bf)
            denc[rows, cols] = (scale * dot(dsc, q, ATB) + dot(pb, t, ATB)).astype(bf)
        send(denc, denc_in, d_send, d_recv, g).start()
        store(0, g).start()
        store(1, g).start()
        return 0

    def back(g, _):
        rows = pl.ds(al(g * ROWS, ROWS), ROWS)
        toks = pl.ds(al(g * CT, CT), CT)
        near = dot(denc[rows, :], wo_ref[own, :], AB)
        send(denc, denc_in, d_send, d_recv, g).wait()
        dmix[...] = (near + dot(denc_in[rows, :], wo_ref[other, :], AB)).astype(bf)
        for h in range(heads):
            cols = slice(h * DH, (h + 1) * DH)
            p = probs[g * heads + h]
            dm = dmix[:, cols]
            gv_ref[toks, cols] = dot(p.astype(bf), dm, AB).astype(bf)
            dpe = dot(v_ref[toks, cols], dm, ABT)
            dse = (p * (dpe - jnp.sum(dpe * p, axis=0, keepdims=True))).astype(bf)
            gk_ref[toks, cols] = (scale * dot(dse, encq[rows, cols], AB)).astype(bf)
        store(2, g).start()
        store(3, g).start()
        return 0

    def both(g, _):
        encode(g, 0)
        return cross(g - 1, 0)

    encode(0, 0)
    lax.fori_loop(1, SPANS, both, 0)
    cross(SPANS - 1, 0)
    for cp in to_sib + to_pair + rq_copies + [fwd] + list(plus.values()) + list(minus.values()) + list(xcopies.values()):
        cp.wait_send()
    for (_, i), cp in ycopies.items():
        if ORDER[i] != (0, 0):
            cp.wait_send()
    for cp in mcopies + [cp for _, _, cp in wy] + ws:
        cp.wait_send()
    lax.fori_loop(0, SPANS, back, 0)
    for n in range(4):
        for g in range(SPANS):
            store(n, g).wait()


def hand_over(*refs):
    inward = [pltpu.make_async_copy(refs[i], refs[8].at[i], refs[9].at[i]) for i in range(4)]
    outward = [pltpu.make_async_copy(refs[8].at[i], refs[4 + i], refs[10].at[i]) for i in range(4)]
    for cp in inward:
        cp.start()
    for i in range(4):
        inward[i].wait()
        outward[i].start()
    for cp in outward:
        cp.wait()


def local(queries, ctx_keys, ctx_values, cotangent, owner, slot_row, database, enc_gain, enc_query_w, enc_out_w):
    dma = pltpu.SemaphoreType.DMA
    bf, f32, i32 = jnp.bfloat16, jnp.float32, jnp.int32
    tokens, half = queries.shape
    full = 2 * half
    rows = SPANS * ROWS
    heads = half // DH
    out = jax.ShapeDtypeStruct((tokens, half), bf)
    vmem, hbm = (pl.BlockSpec(memory_space=sp) for sp in (pltpu.VMEM, pltpu.HBM))
    results = pl.pallas_call(
        kernel,
        out_shape=(out,) * 4,
        in_specs=[hbm, hbm, hbm, vmem] + [hbm] * 6,
        out_specs=(hbm,) * 4,
        scratch_shapes=[
            pltpu.VMEM((tokens, half), bf),
            pltpu.VMEM((tokens, half), bf),
            pltpu.VMEM((tokens, half), bf),
            pltpu.VMEM((tokens, half), bf),
            pltpu.SMEM((K, SPANS), i32),
            pltpu.SMEM((K, SPANS), i32),
            pltpu.VMEM((8, 128), i32),
            pltpu.VMEM((16, 8, 128), i32),
            pltpu.SMEM((16, 8, 128), i32),
            pltpu.VMEM((COL, 2, TOK, 128), bf),
            pltpu.VMEM((2, COL, TOK, 128), bf),
            pltpu.VMEM((64, 2, TOK, 128), bf),
            pltpu.VMEM((64, 2, TOK, 128), bf),
            pltpu.VMEM((8, 2, SPANS, K * TOK, 128), bf),
            pltpu.VMEM((8, SPANS, K * TOK, 128), bf),
            pltpu.VMEM((12, SPANS, ROWS, 128), bf),
            pltpu.VMEM((full, half), bf),
            pltpu.VMEM((full, half), bf),
            pltpu.VMEM((tokens, half), bf),
            pltpu.VMEM((tokens, half), bf),
            pltpu.VMEM((tokens, half), bf),
            pltpu.VMEM((tokens, half), bf),
            pltpu.VMEM((ROWS, full), bf),
            pltpu.VMEM((rows, half), bf),
            pltpu.VMEM((SPANS * heads, CT, ROWS), f32),
            pltpu.VMEM((ROWS, half), bf),
            pltpu.VMEM((rows, half), f32),
            pltpu.VMEM((rows, half), bf),
            pltpu.VMEM((rows, half), bf),
            pltpu.VMEM((rows, half), bf),
            pltpu.VMEM((rows, half), bf),
            pltpu.VMEM((ROWS, half), bf),
            dma((12,)), dma((7,)), dma((7,)), dma((1,)), dma((1,)), dma((3,)), dma((3,)), dma((2,)), dma((2,)),
            dma((14,)), dma((14,)), dma((14,)), dma((14,)),
            dma((2,)), dma((2,)), dma((16,)), dma((16,)), dma((12,)), dma((12,)),
            dma((6,)), dma((6,)), dma((6,)), dma((6,)),
            dma((SPANS,)), dma((SPANS,)), dma((SPANS,)), dma((SPANS,)), dma((4, SPANS)),
        ],
        compiler_params=pltpu.CompilerParams(
            collective_id=0, has_side_effects=True, vmem_limit_bytes=63 * 1024 * 1024),
        cost_estimate=pl.CostEstimate(flops=4_600_000_000, bytes_accessed=12_000_000, transcendentals=600_000),
    )(owner.T, slot_row.T, database, enc_gain, enc_query_w, enc_out_w, queries, ctx_keys, ctx_values, cotangent)
    return pl.pallas_call(
        hand_over,
        out_shape=(out,) * 4,
        in_specs=[hbm] * 4,
        out_specs=(hbm,) * 4,
        scratch_shapes=[pltpu.VMEM((4, tokens, half), bf), dma((4,)), dma((4,))],
        cost_estimate=pl.CostEstimate(flops=0, bytes_accessed=4 * tokens * full, transcendentals=0),
    )(*results)


def solution(mesh):
    tokens = P(("section", "shard"), "mp")
    spans = P(("section", "shard"), None)
    weights = P("section", "mp")
    return jax.shard_map(
        local,
        mesh=mesh,
        in_specs=(tokens,) * 4 + (spans, spans, P("shard", None, None), P(), weights, weights),
        out_specs=(tokens,) * 4,
        check_vma=False,
    )
```

time: 480 us -> 104 us (0.22)
  the two profiles are of different devices: /device:TPU:1 before, /device:TPU:2 now
where the time goes in v3:
time: 104 us
  Pallas kernels  103 us (99%)
    pallas_call x1, Pallas kernels, local(): pl.pallas_call(kernel, out_shape=(out,) * 4, in_specs=[hbm, hbm, hbm, vme...  101 us
    pallas_call x1, Pallas kernels, local(): pl.pallas_call(hand_over, out_shape=(out,) * 4, in_specs=[hbm] * 4, out_s...  2.2 us

profile of v3, /device:TPU:2, one launch (start us, length us, event | category | flops | bytes accessed | tf_op | source)
XLA Modules:
  0.0 103.9 jit_solution(13028000425496865540)
XLA Ops:
  0.6 101.1 %shard_map.129 = (bf16[256,768]{1,0:T(8,128)(2,1)}, bf16[256,768]{1,0:T(8,128)(2,1)}, bf16[256,768]{1,0:T(8,128)(2,1)}, bf16[256,768]{1,0:T(8,128)(2,1)}) custom-call(s32[2,4]{1,0:T(2,128)} %bitcast.2, s32[2,4]{1,0:T(2,128)} %bitcast.3, bf16[12,64,1536]{2,1,0:T(8,128)(2,1)} %db_ref.1, f32[1536]{0:T(1024)} %gain_ref.1, bf16[384,768]{1,0:T(8,128)(2,1)} %wq_hbm.1, ...), custom_call_target="tpu_custom_call" | custom-call | flops 4600000000 | bytes 12000000 | tf_op jit(solution)/shard_map/pallas_call | solution.py:424
  101.7 2.2 %shard_map.130 = (bf16[256,768]{1,0:T(8,128)(2,1)}, bf16[256,768]{1,0:T(8,128)(2,1)}, bf16[256,768]{1,0:T(8,128)(2,1)}, bf16[256,768]{1,0:T(8,128)(2,1)}) custom-call(bf16[256,768]{1,0:T(8,128)(2,1)} %get-tuple-element.8.refs_0_, bf16[256,768]{1,0:T(8,128)(2,1)} %get-tuple-element.9.refs_1_, bf16[256,768]{1,0:T(8,128)(2,1)} %get-tuple-element.10.refs_2_, ...), custom_call_target="tpu_custom_call" | custom-call | bytes 1572864 | tf_op jit(solution)/shard_map/pallas_call | solution.py:472

commit v4 on v3

v4 whole, which is shorter than its diff:
```python
import jax
import jax.numpy as jnp
from jax import lax
from jax.experimental import pallas as pl
from jax.experimental.pallas import tpu as pltpu
from jax.sharding import PartitionSpec as P

DH = 128
CT = 64
NT = 64
K = 2
DB = 12
SPANS = 4
REQ = SPANS * K
TOK = NT // 4
COL = 16 * DB
ROWS = K * NT
MESH = pl.DeviceIdType.MESH
AB = ((1,), (0,))
ABT = ((1,), (1,))
ATB = ((0,), (0,))
ORDER = [(ds, dx) for ds in (2, 1, 3, 0) for dx in (1, 0)]
PEERS = [p for p in ORDER if p != (0, 0)]

def dot(a, b, dims):
    return lax.dot_general(a, b, (dims, ((), ())), preferred_element_type=jnp.float32)


def place(t):
    return (t % 3) * 2 + t // 3


def al(v, n):
    return pl.multiple_of(v, n)


def kernel(owner_hbm, row_hbm, db_ref, gain_ref, wq_hbm, wo_hbm, q_hbm, k_hbm, v_hbm, t_hbm,
           att_hbm, gq_hbm, gk_hbm, gv_hbm,
           att_ref, gq_ref, gk_ref, gv_ref, who, row, req, rq, rqs, gath_0, gath_1, gath_2, xm, f_ref, wq_ref, wo_ref, q_ref, k_ref, v_ref, t_ref,
           normed, encq, probs, mixed, part_own, part_out, part_in, denc, denc_in, dmix,
           loc, rq_send, rq_recv, sib_send, sib_recv, px_send, px_recv,
           zp_send, zp_recv, zm_send, zm_recv, f_send, f_recv,
           wy_send, wy_recv, ws_send, ws_recv, p_send, p_recv, d_send, d_recv, out_sem):
    s = lax.axis_index("section")
    d = lax.axis_index("shard")
    m = lax.axis_index("mp")
    x, z, c = d // 16, (d // 2) % 8, d % 2
    f32, bf = jnp.float32, jnp.bfloat16
    gath = (gath_0, gath_1, gath_2)

    def dev(s_, x_, z_, c_, m_):
        return (s_, x_ * 16 + z_ * 2 + c_, m_)

    def peer(ds, dx, dm=0):
        return dev((s + ds) % 4, (x + dx) % 2, z, c, (m + dm) % 2)

    pair = peer(0, 1)
    up, down = dev(s, x, (z + 1) % 8, c, m), dev(s, x, (z + 7) % 8, c, m)
    mate = dev(s, x, z, c, 1 - m)
    sib = dev(s, x, z, 1 - c, m)
    me = s * 2 + x

    def remote(src, dst, ss, rs, to):
        return pltpu.make_async_remote_copy(src, dst, ss, rs, device_id=to, device_id_type=MESH)

    friends = [peer(*p) for p in PEERS] + [peer(*p, 1) for p in ORDER] + [sib, up, down]
    barrier = pltpu.get_barrier_semaphore()
    for f in friends:
        pl.semaphore_signal(barrier, inc=1, device_id=f, device_id_type=MESH)

    tok = pl.ds(al(s * TOK, TOK), TOK)

    def feat(column, ch):
        return pl.ds(al(((2 * m + column) * 3 + ch) * 128, 128), 128)

    def blocks(zz):
        return pl.ds(zz * 24 + c * DB, DB)

    small = [pltpu.make_async_copy(owner_hbm, who, loc.at[9]), pltpu.make_async_copy(row_hbm, row, loc.at[10])]
    for cp in small:
        cp.start()
    mine, to_pair = [], []
    for ch in range(3):
        cp = pltpu.make_async_copy(db_ref.at[:, tok, feat(x, ch)], gath[ch].at[x, blocks(z)], loc.at[ch])
        cp.start()
        mine.append(cp)
    pl.semaphore_wait(barrier, len(friends))
    for ch in range(3):
        cp = remote(db_ref.at[:, tok, feat(1 - x, ch)], gath[ch].at[x, blocks(z)], px_send.at[ch], px_recv.at[ch], pair)
        cp.start()
        to_pair.append(cp)
    lane = lax.broadcasted_iota(jnp.int32, (8, 128), 1)
    wanted = jnp.zeros((8, 128), jnp.int32)
    for cp in small:
        cp.wait()
    for j in range(REQ):
        g = who[j % K, j // K] * DB + row[j % K, j // K]
        wanted = jnp.where(lane == j, g, wanted)
    req[...] = wanted
    rq[me] = wanted
    rq_copies = []
    for i, p in enumerate(PEERS):
        cp = remote(req, rq.at[me], rq_send.at[i], rq_recv.at[i], peer(*p))
        cp.start()
        rq_copies.append(cp)

    plus, minus, shares = {}, {}, {}

    def zcopy(ch, k, h, up_way):
        zz = (z + 8 - k) % 8 if up_way else (z + k) % 8
        sl = gath[ch].at[(x + h) % 2, blocks(zz)]
        i = ch * 7 + k * 2 + (h if k < 3 else 0)
        if up_way:
            return remote(sl, sl, zp_send.at[i], zp_recv.at[i], up)
        return remote(sl, sl, zm_send.at[i], zm_recv.at[i], down)

    def share(ch, n, zz):
        sl = gath[ch].at[:, blocks(zz)]
        shares[ch, n] = remote(sl, sl, sib_send.at[ch * 8 + n], sib_recv.at[ch * 8 + n], sib)
        shares[ch, n].start()

    def zstep(ch, k, h):
        if k:
            plus[ch, k - 1, h].wait_recv()
            minus[ch, k - 1, h].wait_recv()
        elif h == 0:
            mine[ch].wait()
        else:
            to_pair[ch].wait_recv()
        for way in (True, False):
            if k < 3 or way == (h == 0):
                cp = zcopy(ch, k, h, way)
                cp.start()
                (plus if way else minus)[ch, k, h] = cp
        if h and k:
            share(ch, 2 * k - 1, (z + 8 - k) % 8)
            share(ch, 2 * k, (z + k) % 8)
        elif h:
            share(ch, 0, z)

    def zdone(ch):
        plus[ch, 3, 0].wait_recv()
        minus[ch, 3, 1].wait_recv()
        share(ch, 7, (z + 4) % 8)
        for n in range(8):
            shares[ch, n].wait_recv()

    loads, wy, ws = {}, {}, {}
    wsrc, wdst = (wq_hbm, wo_hbm), (wq_ref, wo_ref)

    def spans_in():
        for i, (src, dst) in enumerate(((q_hbm, q_ref), (k_hbm, k_ref), (v_hbm, v_ref), (t_hbm, t_ref))):
            loads["qkvt"[i]] = pltpu.make_async_copy(src, dst, loc.at[5 + i])
            loads["qkvt"[i]].start()

    def wcopy(w, ds, sec, to):
        part = wdst[w].at[pl.ds(al(sec * 384 + c * 192, 192), 192)]
        src = wsrc[w].at[pl.ds(al(c * 192, 192), 192)] if ds != 2 else part
        i = w * 3 + ds - 1
        return remote(src, part, wy_send.at[i], wy_recv.at[i], peer(to, 0))

    def weights_out(w):
        loads[w] = pltpu.make_async_copy(wsrc[w], wdst[w].at[pl.ds(al(s * 384, 384), 384)], loc.at[3 + w])
        loads[w].start()
        for ds in (1, 3):
            wy[w, ds] = wcopy(w, ds, s, ds)
            wy[w, ds].start()

    def weights_relay():
        for w, ds in ((0, 1), (1, 3)):
            wy[w, ds].wait_recv()
            wy[w, 2] = wcopy(w, 2, (s + 4 - ds) % 4, ds)
            wy[w, 2].start()

    def weights_on(w):
        for ds in (1, 3, 2):
            if (w, ds) not in ((0, 1), (1, 3)):
                wy[w, ds].wait_recv()
            part = wdst[w].at[pl.ds(al(((s + 4 - ds) % 4) * 384 + c * 192, 192), 192)]
            i = w * 3 + ds - 1
            ws[w, ds] = remote(part, part, ws_send.at[i], ws_recv.at[i], sib)
            ws[w, ds].start()

    def weights_here(w):
        loads[w].wait()
        for ds in (1, 3, 2):
            ws[w, ds].wait_recv()

    def requests_in():
        for cp in rq_copies:
            cp.wait_recv()
        cp = pltpu.make_async_copy(rq, rqs, loc.at[11])
        cp.start()
        cp.wait()

    fcopies = {}

    def deliver(ch):
        for i, (ds, dx) in enumerate(ORDER):
            for j in range(REQ):
                g = rqs[((s + ds) % 4) * 2 + (x + dx) % 2, 0, j]
                xm[ch, i, j // K, (j % K) * TOK:(j % K + 1) * TOK] = gath[ch][g // COL, lax.rem(g, COL)]
            src, dst = xm.at[ch, i], f_ref.at[m * 6 + ch * 2 + x, :, pl.ds(al(s * 32, 32), 32), :]
            for dm in (1, 0):
                n = (ch * 8 + i) * 2 + dm
                if (ds, dx, dm) == (0, 0, 0):
                    cp = pltpu.make_async_copy(src, dst, f_recv.at[n])
                else:
                    cp = remote(src, dst, f_send.at[n], f_recv.at[n], peer(ds, dx, dm))
                cp.start()
                fcopies[n] = cp

    def arrived():
        for n, cp in fcopies.items():
            if n % 16 == 14:
                cp.wait()
            else:
                cp.wait_recv()

    for ch in (0, 2, 1):
        zstep(ch, 0, 0)
    weights_out(0)
    weights_out(1)
    zstep(0, 0, 1)
    zstep(0, 1, 0)
    zstep(1, 1, 0)
    zstep(0, 1, 1)
    zstep(0, 2, 0)
    zstep(1, 0, 1)
    zstep(0, 2, 1)
    zstep(2, 0, 1)
    zstep(1, 1, 1)
    requests_in()
    spans_in()
    zstep(0, 3, 0)
    zstep(0, 3, 1)
    zstep(1, 2, 0)
    zstep(1, 2, 1)
    weights_relay()
    zstep(2, 1, 0)
    zstep(2, 1, 1)
    zdone(0)
    deliver(0)
    zstep(1, 3, 0)
    zstep(1, 3, 1)
    zstep(2, 2, 0)
    zstep(2, 2, 1)
    zdone(1)
    deliver(1)
    zstep(2, 3, 0)
    zstep(2, 3, 1)
    zdone(2)
    deliver(2)
    weights_on(0)
    weights_on(1)
    arrived()
    weights_here(0)
    for name in "qkvt":
        loads[name].wait()
    weights_here(1)

    scale = DH ** (-0.5)
    heads = q_ref.shape[1] // DH
    width = heads * DH
    own = pl.ds(al(m * width, 128), width)
    other = pl.ds(al((1 - m) * width, 128), width)

    def send(src, dst, ss, rs, g):
        rows = pl.ds(al(g * ROWS, ROWS), ROWS)
        return remote(src.at[rows], dst.at[rows], ss.at[g], rs.at[g], mate)

    outs = ((att_ref, att_hbm), (gq_ref, gq_hbm), (gk_ref, gk_hbm), (gv_ref, gv_hbm))

    def store(n, g):
        toks = pl.ds(al(g * CT, CT), CT)
        return pltpu.make_async_copy(outs[n][0].at[toks], outs[n][1].at[toks], out_sem.at[n, g])

    def encode(g, _):
        rows = pl.ds(al(g * ROWS, ROWS), ROWS)
        toks = pl.ds(al(g * CT, CT), CT)
        squares = jnp.zeros((ROWS, 128), f32)
        for f in range(12):
            tile = f_ref[f, g].astype(f32)
            squares = squares + tile * tile
        mean = jnp.sum(squares, axis=1, keepdims=True) / (2 * width)
        inv = lax.rsqrt(mean + 1e-06)
        for t in range(12):
            f = (t // 6) * 6 + place(t % 6)
            gain = gain_ref[pl.ds(t * 128, 128)].reshape(1, 128)
            normed[:, t * 128:(t + 1) * 128] = (f_ref[f, g].astype(f32) * inv * gain).astype(bf)
        encq[rows, :] = dot(normed[...], wq_ref[...], AB).astype(bf)
        for h in range(heads):
            cols = slice(h * DH, (h + 1) * DH)
            st = dot(k_ref[toks, cols], encq[rows, cols], ABT) * scale
            e = jnp.exp(st - jnp.max(st, axis=0, keepdims=True))
            p = e / jnp.sum(e, axis=0, keepdims=True)
            probs[g * heads + h] = p
            mixed[:, cols] = dot(p.astype(bf), v_ref[toks, cols], ATB).astype(bf)
        part_out[rows, :] = dot(mixed[...], wo_ref[other, :], ABT).astype(bf)
        send(part_out, part_in, p_send, p_recv, g).start()
        part_own[rows, :] = dot(mixed[...], wo_ref[own, :], ABT)
        return 0

    def cross(g, _):
        rows = pl.ds(al(g * ROWS, ROWS), ROWS)
        toks = pl.ds(al(g * CT, CT), CT)
        send(part_out, part_in, p_send, p_recv, g).wait()
        for h in range(heads):
            cols = slice(h * DH, (h + 1) * DH)
            raw = f_ref[m * 6 + place(h), g].astype(f32)
            enc = (raw + (part_own[rows, cols] + part_in[rows, cols].astype(f32))).astype(bf)
            qt = jnp.concatenate([q_ref[toks, cols], t_ref[toks, cols]], axis=0)
            both = dot(qt, enc, ABT)
            sc, dp = both[:CT] * scale, both[CT:]
            e = jnp.exp(sc - jnp.max(sc, axis=1, keepdims=True))
            p = e / jnp.sum(e, axis=1, keepdims=True)
            dsc = scale * (p * (dp - jnp.sum(dp * p, axis=1, keepdims=True)))
            dsp = jnp.concatenate([dsc.astype(bf), p.astype(bf)], axis=0)
            out = dot(dsp, enc, AB).astype(bf)
            gq_ref[toks, cols] = out[:CT]
            att_ref[toks, cols] = out[CT:]
            denc[rows, cols] = dot(dsp, qt, ATB).astype(bf)
        send(denc, denc_in, d_send, d_recv, g).start()
        store(0, g).start()
        store(1, g).start()
        return 0

    def back(g, _):
        rows = pl.ds(al(g * ROWS, ROWS), ROWS)
        toks = pl.ds(al(g * CT, CT), CT)
        near = dot(denc[rows, :], wo_ref[own, :], AB)
        send(denc, denc_in, d_send, d_recv, g).wait()
        dmix[...] = (near + dot(denc_in[rows, :], wo_ref[other, :], AB)).astype(bf)
        for h in range(heads):
            cols = slice(h * DH, (h + 1) * DH)
            p = probs[g * heads + h]
            dm = dmix[:, cols]
            gv_ref[toks, cols] = dot(p.astype(bf), dm, AB).astype(bf)
            dpe = dot(v_ref[toks, cols], dm, ABT)
            dse = (p * (dpe - jnp.sum(dpe * p, axis=0, keepdims=True))).astype(bf)
            gk_ref[toks, cols] = (scale * dot(dse, encq[rows, cols], AB)).astype(bf)
        store(2, g).start()
        store(3, g).start()
        return 0

    def both(g, _):
        encode(g, 0)
        return cross(g - 1, 0)

    encode(0, 0)
    lax.fori_loop(1, SPANS, both, 0)
    cross(SPANS - 1, 0)
    for cp in to_pair + rq_copies + list(plus.values()) + list(minus.values()) + list(shares.values()):
        cp.wait_send()
    for n, cp in fcopies.items():
        if n % 16 != 14:
            cp.wait_send()
    for cp in list(wy.values()) + list(ws.values()):
        cp.wait_send()
    lax.fori_loop(0, SPANS, back, 0)
    for n in range(4):
        for g in range(SPANS):
            store(n, g).wait()


def hand_over(*refs):
    inward = [pltpu.make_async_copy(refs[i], refs[8].at[i], refs[9].at[i]) for i in range(4)]
    outward = [pltpu.make_async_copy(refs[8].at[i], refs[4 + i], refs[10].at[i]) for i in range(4)]
    for cp in inward:
        cp.start()
    for i in range(4):
        inward[i].wait()
        outward[i].start()
    for cp in outward:
        cp.wait()


def local(queries, ctx_keys, ctx_values, cotangent, owner, slot_row, database, enc_gain, enc_query_w, enc_out_w):
    dma = pltpu.SemaphoreType.DMA
    bf, f32, i32 = jnp.bfloat16, jnp.float32, jnp.int32
    tokens, half = queries.shape
    full = 2 * half
    rows = SPANS * ROWS
    heads = half // DH
    out = jax.ShapeDtypeStruct((tokens, half), bf)
    vmem, hbm = (pl.BlockSpec(memory_space=sp) for sp in (pltpu.VMEM, pltpu.HBM))
    results = pl.pallas_call(
        kernel,
        out_shape=(out,) * 4,
        in_specs=[hbm, hbm, hbm, vmem] + [hbm] * 6,
        out_specs=(hbm,) * 4,
        scratch_shapes=[
            pltpu.VMEM((tokens, half), bf),
            pltpu.VMEM((tokens, half), bf),
            pltpu.VMEM((tokens, half), bf),
            pltpu.VMEM((tokens, half), bf),
            pltpu.SMEM((K, SPANS), i32),
            pltpu.SMEM((K, SPANS), i32),
            pltpu.VMEM((8, 128), i32),
            pltpu.VMEM((8, 8, 128), i32),
            pltpu.SMEM((8, 8, 128), i32),
            pltpu.VMEM((2, COL, TOK, 128), bf),
            pltpu.VMEM((2, COL, TOK, 128), bf),
            pltpu.VMEM((2, COL, TOK, 128), bf),
            pltpu.VMEM((3, 8, SPANS, K * TOK, 128), bf),
            pltpu.VMEM((12, SPANS, ROWS, 128), bf),
            pltpu.VMEM((full, half), bf),
            pltpu.VMEM((full, half), bf),
            pltpu.VMEM((tokens, half), bf),
            pltpu.VMEM((tokens, half), bf),
            pltpu.VMEM((tokens, half), bf),
            pltpu.VMEM((tokens, half), bf),
            pltpu.VMEM((ROWS, full), bf),
            pltpu.VMEM((rows, half), bf),
            pltpu.VMEM((SPANS * heads, CT, ROWS), f32),
            pltpu.VMEM((ROWS, half), bf),
            pltpu.VMEM((rows, half), f32),
            pltpu.VMEM((rows, half), bf),
            pltpu.VMEM((rows, half), bf),
            pltpu.VMEM((rows, half), bf),
            pltpu.VMEM((rows, half), bf),
            pltpu.VMEM((ROWS, half), bf),
            dma((12,)), dma((7,)), dma((7,)), dma((24,)), dma((24,)), dma((3,)), dma((3,)),
            dma((21,)), dma((21,)), dma((21,)), dma((21,)), dma((48,)), dma((48,)),
            dma((6,)), dma((6,)), dma((6,)), dma((6,)),
            dma((SPANS,)), dma((SPANS,)), dma((SPANS,)), dma((SPANS,)), dma((4, SPANS)),
        ],
        compiler_params=pltpu.CompilerParams(
            collective_id=0, has_side_effects=True, vmem_limit_bytes=63 * 1024 * 1024),
        cost_estimate=pl.CostEstimate(flops=4_600_000_000, bytes_accessed=12_000_000, transcendentals=600_000),
    )(owner.T, slot_row.T, database, enc_gain, enc_query_w, enc_out_w, queries, ctx_keys, ctx_values, cotangent)
    return pl.pallas_call(
        hand_over,
        out_shape=(out,) * 4,
        in_specs=[hbm] * 4,
        out_specs=(hbm,) * 4,
        scratch_shapes=[pltpu.VMEM((4, tokens, half), bf), dma((4,)), dma((4,))],
        cost_estimate=pl.CostEstimate(flops=0, bytes_accessed=4 * tokens * full, transcendentals=0),
    )(*results)


def solution(mesh):
    tokens = P(("section", "shard"), "mp")
    spans = P(("section", "shard"), None)
    weights = P("section", "mp")
    return jax.shard_map(
        local,
        mesh=mesh,
        in_specs=(tokens,) * 4 + (spans, spans, P("shard", None, None), P(), weights, weights),
        out_specs=(tokens,) * 4,
        check_vma=False,
    )
```

time: 104 us -> 99.1 us (0.953)
  the two profiles are of different devices: /device:TPU:2 before, /device:TPU:1 now
where the time goes in v4:
time: 99.1 us; the launch traced here: 99 us
  Pallas kernels  98.3 us (99%)
    pallas_call x1, Pallas kernels, local(): pl.pallas_call(kernel, out_shape=(out,) * 4, in_specs=[hbm, hbm, hbm, vme...  96.1 us
    pallas_call x1, Pallas kernels, local(): pl.pallas_call(hand_over, out_shape=(out,) * 4, in_specs=[hbm] * 4, out_s...  2.2 us

profile of v4, /device:TPU:1, one launch (start us, length us, event | category | flops | bytes accessed | tf_op | source)
XLA Modules:
  0.0 99.0 jit_solution(2094442379509248849)
XLA Ops:
  0.6 96.1 %shard_map.129 = (bf16[256,768]{1,0:T(8,128)(2,1)}, bf16[256,768]{1,0:T(8,128)(2,1)}, bf16[256,768]{1,0:T(8,128)(2,1)}, bf16[256,768]{1,0:T(8,128)(2,1)}) custom-call(s32[2,4]{1,0:T(2,128)} %bitcast.2, s32[2,4]{1,0:T(2,128)} %bitcast.3, bf16[12,64,1536]{2,1,0:T(8,128)(2,1)} %db_ref.1, f32[1536]{0:T(1024)} %gain_ref.1, bf16[384,768]{1,0:T(8,128)(2,1)} %wq_hbm.1, ...), custom_call_target="tpu_custom_call" | custom-call | flops 4600000000 | bytes 12000000 | tf_op jit(solution)/shard_map/pallas_call | solution.py:387
  96.8 2.2 %shard_map.130 = (bf16[256,768]{1,0:T(8,128)(2,1)}, bf16[256,768]{1,0:T(8,128)(2,1)}, bf16[256,768]{1,0:T(8,128)(2,1)}, bf16[256,768]{1,0:T(8,128)(2,1)}) custom-call(bf16[256,768]{1,0:T(8,128)(2,1)} %get-tuple-element.8.refs_0_, bf16[256,768]{1,0:T(8,128)(2,1)} %get-tuple-element.9.refs_1_, bf16[256,768]{1,0:T(8,128)(2,1)} %get-tuple-element.10.refs_2_, ...), custom_call_target="tpu_custom_call" | custom-call | bytes 1572864 | tf_op jit(solution)/shard_map/pallas_call | solution.py:432

commit v5 on v4

--- a/solution.py
+++ b/solution.py
@@ -37,10 +37,10 @@
 def kernel(owner_hbm, row_hbm, db_ref, gain_ref, wq_hbm, wo_hbm, q_hbm, k_hbm, v_hbm, t_hbm,
            att_hbm, gq_hbm, gk_hbm, gv_hbm,
            att_ref, gq_ref, gk_ref, gv_ref, who, row, req, rq, rqs, gath_0, gath_1, gath_2, xm, f_ref, wq_ref, wo_ref, q_ref, k_ref, v_ref, t_ref,
-           normed, encq, probs, mixed, part_own, part_out, part_in, denc, denc_in, dmix,
+           normed, encq, probs, pb_out, pb_in, v2_ref, w2_ref, mixed, part_own, denc, denc_in, dmix,
            loc, rq_send, rq_recv, sib_send, sib_recv, px_send, px_recv,
            zp_send, zp_recv, zm_send, zm_recv, f_send, f_recv,
-           wy_send, wy_recv, ws_send, ws_recv, p_send, p_recv, d_send, d_recv, out_sem):
+           wy_send, wy_recv, ws_send, ws_recv, v_send, v_recv, w2_send, w2_recv, w2s_send, w2s_recv, p_send, p_recv, d_send, d_recv, out_sem):
     s = lax.axis_index("section")
     d = lax.axis_index("shard")
     m = lax.axis_index("mp")
@@ -186,6 +186,74 @@
         for ds in (1, 3, 2):
             ws[w, ds].wait_recv()
 
+    v_out = remote(v_hbm, v2_ref, v_send.at[0], v_recv.at[0], mate)
+
+    def w2_rows(u):
+        return w2_ref.at[pl.ds(al(u * 384 + c * 192, 192), 192)]
+
+    role = (s + 4 - 2 * m) % 4
+    first = ((role + 1) // 2) % 2
+
+    def w2_first():
+        return remote(wo_hbm.at[pl.ds(al(c * 192, 192), 192)], w2_rows(s % 2), w2_send.at[0], w2_recv.at[s % 2], mate)
+
+    def w2_next(ds):
+        return remote(w2_rows(first), w2_rows(first), w2_send.at[ds], w2_recv.at[first], peer(ds, 0))
+
+    def w2_wait(u):
+        remote(w2_rows(u), w2_rows(u), w2_send.at[0], w2_recv.at[u], mate).wait_recv()
+
+    def w2_sib(u):
+        return remote(w2_rows(u), w2_rows(u), w2s_send.at[u], w2s_recv.at[u], sib)
+
+    def others_out():
+        @pl.when(s // 2 == 1 - m)
+        def _():
+            w2_first().start()
+
+    def w2_spread():
+        @pl.when(role < 2)
+        def _():
+            w2_wait(first)
+            w2_next(1).start()
+            w2_next(3).start()
+
+    def w2_relay():
+        @pl.when(role == 2)
+        def _():
+            w2_wait(first)
+            w2_next(1).start()
+
+        @pl.when(role == 3)
+        def _():
+            w2_wait(first)
+            w2_next(3).start()
+
+    def w2_on():
+        w2_sib(first).start()
+        w2_wait(1 - first)
+        w2_sib(1 - first).start()
+
+    def w2_here():
+        for u in range(2):
+            w2_sib(u).wait_recv()
+
+    def w2_sent():
+        @pl.when(s // 2 == 1 - m)
+        def _():
+            w2_first().wait_send()
+
+        @pl.when(role != 3)
+        def _():
+            w2_next(1).wait_send()
+
+        @pl.when(role != 2)
+        def _():
+            w2_next(3).wait_send()
+
+        for u in range(2):
+            w2_sib(u).wait_send()
+
     def requests_in():
         for cp in rq_copies:
             cp.wait_recv()
@@ -195,14 +263,17 @@
 
     fcopies = {}
 
-    def deliver(ch):
+    def deliver(ch, spans=(0, SPANS), base=None):
+        base = ch * 16 if base is None else base
+        some = pl.ds(spans[0], spans[1] - spans[0])
         for i, (ds, dx) in enumerate(ORDER):
-            for j in range(REQ):
+            for j in range(spans[0] * K, spans[1] * K):
                 g = rqs[((s + ds) % 4) * 2 + (x + dx) % 2, 0, j]
                 xm[ch, i, j // K, (j % K) * TOK:(j % K + 1) * TOK] = gath[ch][g // COL, lax.rem(g, COL)]
-            src, dst = xm.at[ch, i], f_ref.at[m * 6 + ch * 2 + x, :, pl.ds(al(s * 32, 32), 32), :]
+            src = xm.at[ch, i, some]
+            dst = f_ref.at[m * 6 + ch * 2 + x, some, pl.ds(al(s * 32, 32), 32), :]
             for dm in (1, 0):
-                n = (ch * 8 + i) * 2 + dm
+                n = base + i * 2 + dm
                 if (ds, dx, dm) == (0, 0, 0):
                     cp = pltpu.make_async_copy(src, dst, f_recv.at[n])
                 else:
@@ -210,16 +281,17 @@
                 cp.start()
                 fcopies[n] = cp
 
-    def arrived():
-        for n, cp in fcopies.items():
+    def arrived(first, last):
+        for n in range(first, last):
             if n % 16 == 14:
-                cp.wait()
+                fcopies[n].wait()
             else:
-                cp.wait_recv()
+                fcopies[n].wait_recv()
 
     for ch in (0, 2, 1):
         zstep(ch, 0, 0)
     weights_out(0)
+    others_out()
     weights_out(1)
     zstep(0, 0, 1)
     zstep(0, 1, 0)
@@ -232,10 +304,12 @@
     zstep(1, 1, 1)
     requests_in()
     spans_in()
+    v_out.start()
     zstep(0, 3, 0)
     zstep(0, 3, 1)
     zstep(1, 2, 0)
     zstep(1, 2, 1)
+    w2_spread()
     weights_relay()
     zstep(2, 1, 0)
     zstep(2, 1, 1)
@@ -250,14 +324,14 @@
     zstep(2, 3, 0)
     zstep(2, 3, 1)
     zdone(2)
-    deliver(2)
+    deliver(2, (0, 2), 32)
+    deliver(2, (2, 4), 48)
+    w2_relay()
     weights_on(0)
-    weights_on(1)
-    arrived()
+    arrived(0, 48)
     weights_here(0)
     for name in "qkvt":
         loads[name].wait()
-    weights_here(1)
 
     scale = DH ** (-0.5)
     heads = q_ref.shape[1] // DH
@@ -274,6 +348,10 @@
     def store(n, g):
         toks = pl.ds(al(g * CT, CT), CT)
         return pltpu.make_async_copy(outs[n][0].at[toks], outs[n][1].at[toks], out_sem.at[n, g])
+
+    def send_p(g):
+        part = pl.ds(g * heads, heads)
+        return remote(pb_out.at[part], pb_in.at[part], p_send.at[g], p_recv.at[g], mate)
 
     def encode(g, _):
         rows = pl.ds(al(g * ROWS, ROWS), ROWS)
@@ -295,20 +373,26 @@
             e = jnp.exp(st - jnp.max(st, axis=0, keepdims=True))
             p = e / jnp.sum(e, axis=0, keepdims=True)
             probs[g * heads + h] = p
-            mixed[:, cols] = dot(p.astype(bf), v_ref[toks, cols], ATB).astype(bf)
-        part_out[rows, :] = dot(mixed[...], wo_ref[other, :], ABT).astype(bf)
-        send(part_out, part_in, p_send, p_recv, g).start()
-        part_own[rows, :] = dot(mixed[...], wo_ref[own, :], ABT)
+            pb_out[g * heads + h] = p.astype(bf)
+        send_p(g).start()
         return 0
 
     def cross(g, _):
         rows = pl.ds(al(g * ROWS, ROWS), ROWS)
         toks = pl.ds(al(g * CT, CT), CT)
-        send(part_out, part_in, p_send, p_recv, g).wait()
+        for h in range(heads):
+            cols = slice(h * DH, (h + 1) * DH)
+            mixed[:, cols] = dot(pb_out[g * heads + h], v_ref[toks, cols], ATB).astype(bf)
+        part_own[...] = dot(mixed[...], wo_ref[own, :], ABT)
+        send_p(g).wait()
+        for h in range(heads):
+            cols = slice(h * DH, (h + 1) * DH)
+            mixed[:, cols] = dot(pb_in[g * heads + h], v2_ref[toks, cols], ATB).astype(bf)
+        part_own[...] += dot(mixed[...], w2_ref[...], ABT)
         for h in range(heads):
             cols = slice(h * DH, (h + 1) * DH)
             raw = f_ref[m * 6 + place(h), g].astype(f32)
-            enc = (raw + (part_own[rows, cols] + part_in[rows, cols].astype(f32))).astype(bf)
+            enc = (raw + part_own[:, cols]).astype(bf)
             qt = jnp.concatenate([q_ref[toks, cols], t_ref[toks, cols]], axis=0)
             both = dot(qt, enc, ABT)
             sc, dp = both[:CT] * scale, both[CT:]
@@ -345,18 +429,26 @@
 
     def both(g, _):
         encode(g, 0)
-        return cross(g - 1, 0)
+        return cross(g - 2, 0)
 
     encode(0, 0)
-    lax.fori_loop(1, SPANS, both, 0)
-    cross(SPANS - 1, 0)
+    encode(1, 0)
+    weights_on(1)
+    w2_on()
+    weights_here(1)
+    w2_here()
+    v_out.wait_recv()
+    arrived(48, 64)
+    lax.fori_loop(2, SPANS, both, 0)
+    lax.fori_loop(SPANS - 2, SPANS, cross, 0)
     for cp in to_pair + rq_copies + list(plus.values()) + list(minus.values()) + list(shares.values()):
         cp.wait_send()
     for n, cp in fcopies.items():
         if n % 16 != 14:
             cp.wait_send()
-    for cp in list(wy.values()) + list(ws.values()):
+    for cp in list(wy.values()) + list(ws.values()) + [v_out]:
         cp.wait_send()
+    w2_sent()
     lax.fori_loop(0, SPANS, back, 0)
     for n in range(4):
         for g in range(SPANS):
@@ -413,16 +505,19 @@
             pltpu.VMEM((ROWS, full), bf),
             pltpu.VMEM((rows, half), bf),
             pltpu.VMEM((SPANS * heads, CT, ROWS), f32),
+            pltpu.VMEM((SPANS * heads, CT, ROWS), bf),
+            pltpu.VMEM((SPANS * heads, CT, ROWS), bf),
+            pltpu.VMEM((tokens, half), bf),
+            pltpu.VMEM((half, half), bf),
             pltpu.VMEM((ROWS, half), bf),
-            pltpu.VMEM((rows, half), f32),
-            pltpu.VMEM((rows, half), bf),
-            pltpu.VMEM((rows, half), bf),
+            pltpu.VMEM((ROWS, half), f32),
             pltpu.VMEM((rows, half), bf),
             pltpu.VMEM((rows, half), bf),
             pltpu.VMEM((ROWS, half), bf),
             dma((12,)), dma((7,)), dma((7,)), dma((24,)), dma((24,)), dma((3,)), dma((3,)),
-            dma((21,)), dma((21,)), dma((21,)), dma((21,)), dma((48,)), dma((48,)),
+            dma((21,)), dma((21,)), dma((21,)), dma((21,)), dma((64,)), dma((64,)),
             dma((6,)), dma((6,)), dma((6,)), dma((6,)),
+            dma((1,)), dma((1,)), dma((4,)), dma((2,)), dma((2,)), dma((2,)),
             dma((SPANS,)), dma((SPANS,)), dma((SPANS,)), dma((SPANS,)), dma((4, SPANS)),
         ],
         compiler_params=pltpu.CompilerParams(

time: 99.1 us -> 96.4 us (0.973)
  Pallas kernels: 98.3 us -> 95.6 us
    pallas_call x1, Pallas kernels: 96.1 us -> 93.4 us  [local(): pl.pallas_call(kernel, out_shape=(out,) * 4, in_specs=[hbm, hbm, hbm, vme...]
where the time goes in v5:
time: 96.4 us; the launch traced here: 96.2 us
  Pallas kernels  95.6 us (99%)
    pallas_call x1, Pallas kernels, local(): pl.pallas_call(kernel, out_shape=(out,) * 4, in_specs=[hbm, hbm, hbm, vme...  93.4 us
    pallas_call x1, Pallas kernels, local(): pl.pallas_call(hand_over, out_shape=(out,) * 4, in_specs=[hbm] * 4, out_s...  2.2 us

profile of v5, /device:TPU:1, one launch (start us, length us, event | category | flops | bytes accessed | tf_op | source)
XLA Modules:
  0.0 96.2 jit_solution(1111991668589621148)
XLA Ops:
  0.6 93.4 %shard_map.129 = (bf16[256,768]{1,0:T(8,128)(2,1)}, bf16[256,768]{1,0:T(8,128)(2,1)}, bf16[256,768]{1,0:T(8,128)(2,1)}, bf16[256,768]{1,0:T(8,128)(2,1)}) custom-call(s32[2,4]{1,0:T(2,128)} %bitcast.2, s32[2,4]{1,0:T(2,128)} %bitcast.3, bf16[12,64,1536]{2,1,0:T(8,128)(2,1)} %db_ref.1, f32[1536]{0:T(1024)} %gain_ref.1, bf16[384,768]{1,0:T(8,128)(2,1)} %wq_hbm.1, ...), custom_call_target="tpu_custom_call" | custom-call | flops 4600000000 | bytes 12000000 | tf_op jit(solution)/shard_map/pallas_call | solution.py:479
  94.0 2.2 %shard_map.130 = (bf16[256,768]{1,0:T(8,128)(2,1)}, bf16[256,768]{1,0:T(8,128)(2,1)}, bf16[256,768]{1,0:T(8,128)(2,1)}, bf16[256,768]{1,0:T(8,128)(2,1)}) custom-call(bf16[256,768]{1,0:T(8,128)(2,1)} %get-tuple-element.8.refs_0_, bf16[256,768]{1,0:T(8,128)(2,1)} %get-tuple-element.9.refs_1_, bf16[256,768]{1,0:T(8,128)(2,1)} %get-tuple-element.10.refs_2_, ...), custom_call_target="tpu_custom_call" | custom-call | bytes 1572864 | tf_op jit(solution)/shard_map/pallas_call | solution.py:527

commit v6 on v5

--- a/solution.py
+++ b/solution.py
@@ -166,11 +166,11 @@
             wy[w, ds] = wcopy(w, ds, s, ds)
             wy[w, ds].start()
 
-    def weights_relay():
-        for w, ds in ((0, 1), (1, 3)):
-            wy[w, ds].wait_recv()
-            wy[w, 2] = wcopy(w, 2, (s + 4 - ds) % 4, ds)
-            wy[w, 2].start()
+    def weights_relay(w):
+        ds = (1, 3)[w]
+        wy[w, ds].wait_recv()
+        wy[w, 2] = wcopy(w, 2, (s + 4 - ds) % 4, ds)
+        wy[w, 2].start()
 
     def weights_on(w):
         for ds in (1, 3, 2):
@@ -304,13 +304,14 @@
     zstep(1, 1, 1)
     requests_in()
     spans_in()
+    weights_relay(0)
+    w2_spread()
     v_out.start()
     zstep(0, 3, 0)
     zstep(0, 3, 1)
     zstep(1, 2, 0)
     zstep(1, 2, 1)
-    w2_spread()
-    weights_relay()
+    weights_relay(1)
     zstep(2, 1, 0)
     zstep(2, 1, 1)
     zdone(0)
@@ -339,9 +340,9 @@
     own = pl.ds(al(m * width, 128), width)
     other = pl.ds(al((1 - m) * width, 128), width)
 
-    def send(src, dst, ss, rs, g):
-        rows = pl.ds(al(g * ROWS, ROWS), ROWS)
-        return remote(src.at[rows], dst.at[rows], ss.at[g], rs.at[g], mate)
+    def send_d(g, part):
+        block = (pl.ds(al(g * ROWS, ROWS), ROWS), slice(part * (width // 2), (part + 1) * (width // 2)))
+        return remote(denc.at[block], denc_in.at[block], d_send.at[g, part], d_recv.at[g, part], mate)
 
     outs = ((att_ref, att_hbm), (gq_ref, gq_hbm), (gk_ref, gk_hbm), (gv_ref, gv_hbm))
 
@@ -371,7 +372,7 @@
             cols = slice(h * DH, (h + 1) * DH)
             st = dot(k_ref[toks, cols], encq[rows, cols], ABT) * scale
             e = jnp.exp(st - jnp.max(st, axis=0, keepdims=True))
-            p = e / jnp.sum(e, axis=0, keepdims=True)
+            p = e * (1.0 / jnp.sum(e, axis=0, keepdims=True))
             probs[g * heads + h] = p
             pb_out[g * heads + h] = p.astype(bf)
         send_p(g).start()
@@ -397,14 +398,15 @@
             both = dot(qt, enc, ABT)
             sc, dp = both[:CT] * scale, both[CT:]
             e = jnp.exp(sc - jnp.max(sc, axis=1, keepdims=True))
-            p = e / jnp.sum(e, axis=1, keepdims=True)
+            p = e * (1.0 / jnp.sum(e, axis=1, keepdims=True))
             dsc = scale * (p * (dp - jnp.sum(dp * p, axis=1, keepdims=True)))
             dsp = jnp.concatenate([dsc.astype(bf), p.astype(bf)], axis=0)
             out = dot(dsp, enc, AB).astype(bf)
             gq_ref[toks, cols] = out[:CT]
             att_ref[toks, cols] = out[CT:]
             denc[rows, cols] = dot(dsp, qt, ATB).astype(bf)
-        send(denc, denc_in, d_send, d_recv, g).start()
+            if h % 3 == 2:
+                send_d(g, h // 3).start()
         store(0, g).start()
         store(1, g).start()
         return 0
@@ -413,7 +415,8 @@
         rows = pl.ds(al(g * ROWS, ROWS), ROWS)
         toks = pl.ds(al(g * CT, CT), CT)
         near = dot(denc[rows, :], wo_ref[own, :], AB)
-        send(denc, denc_in, d_send, d_recv, g).wait()
+        send_d(g, 0).wait()
+        send_d(g, 1).wait()
         dmix[...] = (near + dot(denc_in[rows, :], wo_ref[other, :], AB)).astype(bf)
         for h in range(heads):
             cols = slice(h * DH, (h + 1) * DH)
@@ -518,7 +521,7 @@
             dma((21,)), dma((21,)), dma((21,)), dma((21,)), dma((64,)), dma((64,)),
             dma((6,)), dma((6,)), dma((6,)), dma((6,)),
             dma((1,)), dma((1,)), dma((4,)), dma((2,)), dma((2,)), dma((2,)),
-            dma((SPANS,)), dma((SPANS,)), dma((SPANS,)), dma((SPANS,)), dma((4, SPANS)),
+            dma((SPANS,)), dma((SPANS,)), dma((SPANS, 2)), dma((SPANS, 2)), dma((4, SPANS)),
         ],
         compiler_params=pltpu.CompilerParams(
             collective_id=0, has_side_effects=True, vmem_limit_bytes=63 * 1024 * 1024),

time: 96.4 us -> 92.9 us (0.964)
  Pallas kernels: 95.6 us -> 92.1 us
    pallas_call x1, Pallas kernels: 93.4 us -> 89.9 us  [local(): pl.pallas_call(kernel, out_shape=(out,) * 4, in_specs=[hbm, hbm, hbm, vme...]
where the time goes in v6:
time: 92.9 us; the launch traced here: 92.7 us
  Pallas kernels  92.1 us (99%)
    pallas_call x1, Pallas kernels, local(): pl.pallas_call(kernel, out_shape=(out,) * 4, in_specs=[hbm, hbm, hbm, vme...  89.9 us
    pallas_call x1, Pallas kernels, local(): pl.pallas_call(hand_over, out_shape=(out,) * 4, in_specs=[hbm] * 4, out_s...  2.2 us

profile of v6, /device:TPU:1, one launch (start us, length us, event | category | flops | bytes accessed | tf_op | source)
XLA Modules:
  0.0 92.7 jit_solution(5091290872975088502)
XLA Ops:
  0.6 89.9 %shard_map.129 = (bf16[256,768]{1,0:T(8,128)(2,1)}, bf16[256,768]{1,0:T(8,128)(2,1)}, bf16[256,768]{1,0:T(8,128)(2,1)}, bf16[256,768]{1,0:T(8,128)(2,1)}) custom-call(s32[2,4]{1,0:T(2,128)} %bitcast.2, s32[2,4]{1,0:T(2,128)} %bitcast.3, bf16[12,64,1536]{2,1,0:T(8,128)(2,1)} %db_ref.1, f32[1536]{0:T(1024)} %gain_ref.1, bf16[384,768]{1,0:T(8,128)(2,1)} %wq_hbm.1, ...), custom_call_target="tpu_custom_call" | custom-call | flops 4600000000 | bytes 12000000 | tf_op jit(solution)/shard_map/pallas_call | solution.py:482
  90.5 2.2 %shard_map.130 = (bf16[256,768]{1,0:T(8,128)(2,1)}, bf16[256,768]{1,0:T(8,128)(2,1)}, bf16[256,768]{1,0:T(8,128)(2,1)}, bf16[256,768]{1,0:T(8,128)(2,1)}) custom-call(bf16[256,768]{1,0:T(8,128)(2,1)} %get-tuple-element.8.refs_0_, bf16[256,768]{1,0:T(8,128)(2,1)} %get-tuple-element.9.refs_1_, bf16[256,768]{1,0:T(8,128)(2,1)} %get-tuple-element.10.refs_2_, ...), custom_call_target="tpu_custom_call" | custom-call | bytes 1572864 | tf_op jit(solution)/shard_map/pallas_call | solution.py:530
